TPU v7x, 32 devices: a whole 2x2x4 slice. The times are simulated.
32 devices in a mesh: morton: 4 (over z), slab: 8 (over y, x, core).
Axes of the slice: x: 2, y: 2, z: 4, core: 2. Of those that a mesh axis runs over, the one named last changes fastest.
Arguments:
- velocity: float32 [128, 64, 256], P('slab', 'morton'), may hold values from -6 to 6
Outputs:
- approx: float32 [32, 16, 64], P('slab', 'morton')
- detail_two: float32 [7, 32, 16, 64], P(None, 'slab', 'morton')
- detail_one: float32 [7, 64, 32, 128], P(None, 'slab', 'morton')
All inputs are finite; a program needn't handle non-finite values.
Results may differ from a plain program's by a relative error of at most 0.00002.
Values sent between devices are 32-bit elements; how exact they have to be, the bound alone decides.
A program may use at most 64 MiB of HBM per device.

v0:
```python
import jax
import jax.numpy as jnp
from jax import lax
from jax.sharding import PartitionSpec as P

LIFT_ALPHA = -1.586134342059924
LIFT_BETA = -0.052980118572961
LIFT_GAMMA = 0.882911075530934
LIFT_DELTA = 0.443506852043971
LIFT_SCALE = 1.149604398860241


def extended_2(x, sides, width):
    for axis, dim in sides:
        devices, length = (lax.axis_size(axis), x.shape[dim])
        up = [(i, (i + 1) % devices) for i in range(devices - 1)]
        down = [(j, i) for i, j in up]
        last = lax.slice_in_dim(x, length - width, length, axis=dim)
        initial = lax.slice_in_dim(x, 0, width, axis=dim)
        before = lax.ppermute(last, axis, up)
        after = lax.ppermute(initial, axis, down)
        x = jnp.concatenate([before, x, after], axis=dim)
    return x


def cut_range(values, start, stop, dimension):
    return lax.slice_in_dim(values, start, stop, axis=dimension)


def lifting(extended, dimension):
    halfway = extended.shape[dimension] // 2
    new_shape = extended.shape[:dimension] + (halfway, 2) + extended.shape[dimension + 1 :]
    paired = extended.reshape(new_shape)
    even_part = lax.index_in_dim(paired, 0, dimension + 1, keepdims=False)
    odd_part = lax.index_in_dim(paired, 1, dimension + 1, keepdims=False)
    first_detail = cut_range(odd_part, 0, halfway - 1, dimension) + LIFT_ALPHA * (
        cut_range(even_part, 0, halfway - 1, dimension)
        + cut_range(even_part, 1, halfway, dimension)
    )
    first_smooth = cut_range(even_part, 1, halfway - 1, dimension) + LIFT_BETA * (
        cut_range(first_detail, 0, halfway - 2, dimension)
        + cut_range(first_detail, 1, halfway - 1, dimension)
    )
    second_detail = cut_range(first_detail, 1, halfway - 2, dimension) + LIFT_GAMMA * (
        cut_range(first_smooth, 0, halfway - 3, dimension)
        + cut_range(first_smooth, 1, halfway - 2, dimension)
    )
    second_smooth = cut_range(first_smooth, 1, halfway - 3, dimension) + LIFT_DELTA * (
        cut_range(second_detail, 0, halfway - 4, dimension)
        + cut_range(second_detail, 1, halfway - 3, dimension)
    )
    lowpass = second_smooth * LIFT_SCALE
    highpass = cut_range(second_detail, 1, halfway - 3, dimension) / LIFT_SCALE
    return (lowpass, highpass)


def reflect_edges(extended, dimension, margin, at_low, at_high):
    length = extended.shape[dimension]
    low_mirror = jnp.flip(cut_range(extended, margin + 1, 2 * margin + 1, dimension), dimension)
    high_mirror = jnp.flip(
        cut_range(extended, length - 2 * margin - 1, length - margin - 1, dimension), dimension
    )
    leading = jnp.where(at_low, low_mirror, cut_range(extended, 0, margin, dimension))
    trailing = jnp.where(
        at_high, high_mirror, cut_range(extended, length - margin, length, dimension)
    )
    middle = cut_range(extended, margin, length - margin, dimension)
    return jnp.concatenate([leading, middle, trailing], axis=dimension)


def split_depth(planar):
    subbands = []
    for x_band in planar:
        padded = jnp.pad(x_band, ((0, 0), (0, 0), (4, 4)), mode="reflect")
        lowpass, highpass = lifting(padded, 2)
        subbands = subbands + [lowpass, highpass]
    return subbands


def split_plane(extended):
    planar = []
    for x_band in lifting(extended, 0):
        lowpass, highpass = lifting(x_band, 1)
        planar = planar + [lowpass, highpass]
    return planar


def per_device(velocity):
    slab_low = lax.axis_index("slab") == 0
    slab_high = lax.axis_index("slab") == lax.axis_size("slab") - 1
    morton_low = lax.axis_index("morton") == 0
    morton_high = lax.axis_index("morton") == lax.axis_size("morton") - 1
    margin = 4
    extended = extended_2(velocity, (("slab", 0),), margin)
    extended = reflect_edges(extended, 0, margin, slab_low, slab_high)
    lowpass, highpass = lifting(extended, 0)
    stacked = jnp.stack([lowpass, highpass])
    widened = extended_2(stacked, (("morton", 2),), margin)
    widened = reflect_edges(widened, 2, margin, morton_low, morton_high)
    low_rows, high_rows = lifting(widened, 2)
    planar = [low_rows[0], high_rows[0], low_rows[1], high_rows[1]]
    level_one = split_depth(planar)
    detail_one = jnp.stack([subband for subband in level_one[1:]])
    coarse = extended_2(level_one[0], (("morton", 1), ("slab", 0)), 4)
    coarse = reflect_edges(coarse, 0, 4, slab_low, slab_high)
    coarse = reflect_edges(coarse, 1, 4, morton_low, morton_high)
    level_two = split_depth(split_plane(coarse))
    return (level_two[0], jnp.stack(level_two[1:]), detail_one)


def solution(mesh):
    placed = (P("slab", "morton", None),)
    return jax.shard_map(
        per_device,
        mesh=mesh,
        in_specs=placed,
        out_specs=(
            P("slab", "morton", None),
            P(None, "slab", "morton", None),
            P(None, "slab", "morton", None),
        ),
        check_vma=False,
    )
```

profile of v0, /device:TPU:4, one launch (start us, length us, event | category | flops | bytes accessed | tf_op | source)
XLA Modules:
  0.0 62.3 jit_solution(2056143983983537617)
XLA Ops:
  0.6 1.0 %fusion.132 = (f32[4,16,256]{2,1,0:T(8,128)S(1)}, f32[4,16,256]{2,1,0:T(8,128)S(1)}, f32[4,16,256]{2,1,0:T(8,128)S(1)}, f32[4,16,256]{2,1,0:T(8,128)S(1)}) fusion(f32[16,16,256]{2,1,0:T(8,128)} %param.1), kind=kLoop, calls=%fused_computation.249 | loop fusion | bytes 524288 | tf_op jit(solution)/shard_map/slice | solution.py:27
  1.6 1.9 %collective-permute-start = (f32[4,16,256]{2,1,0:T(8,128)S(1)}, f32[4,16,256]{2,1,0:T(8,128)S(1)}, u32[]{:S(2)}, u32[]{:S(2)}) collective-permute-start(f32[4,16,256]{2,1,0:T(8,128)S(1)} %get-tuple-element.46), channel_id=1, source_target_pairs={{0,1},{1,2},{2,3},{3,4},{4,5},{5,6},{6,7},{8,9},{9,10},{10,11},{11... | collective-permute-start | bytes 196616 | tf_op jit(solution)/shard_map/ppermute | solution.py:20
  3.6 4.5 %collective-permute-start.1 = (f32[4,16,256]{2,1,0:T(8,128)S(1)}, f32[4,16,256]{2,1,0:T(8,128)S(1)}, u32[]{:S(2)}, u32[]{:S(2)}) collective-permute-start(f32[4,16,256]{2,1,0:T(8,128)S(1)} %get-tuple-element.47), channel_id=1, source_target_pairs={{1,0},{2,1},{3,2},{4,3},{5,4},{6,5},{7,6},{9,8},{10,9},{11,10},{12... | collective-permute-start | bytes 196616 | tf_op jit(solution)/shard_map/ppermute | solution.py:21
  8.2 1.8 %collective-permute-done.1 = f32[4,16,256]{2,1,0:T(8,128)S(1)} collective-permute-done((f32[4,16,256]{2,1,0:T(8,128)S(1)}, f32[4,16,256]{2,1,0:T(8,128)S(1)}, u32[]{:S(2)}, u32[]{:S(2)}) %collective-permute-start.1) | collective-permute-done | bytes 65568 | tf_op jit(solution)/shard_map/ppermute | solution.py:21
  10.3 3.5 %collective-permute-start.2 = (f32[2,8,4,256]{3,2,1,0:T(4,128)S(1)}, f32[2,8,4,256]{3,2,1,0:T(4,128)S(1)}, u32[]{:S(2)}, u32[]{:S(2)}) collective-permute-start(f32[2,8,4,256]{3,2,1,0:T(4,128)S(1)} %get-tuple-element.40), channel_id=1, source_target_pairs={{0,8},{8,16},{16,24},{1,9},{9,17},{17,25},{2,10},{10,18},{18,26},{... | collective-permute-start | bytes 196616 | tf_op jit(solution)/shard_map/ppermute | solution.py:20
  13.8 0.2 rev.84
  13.9 0.2 rev.85
  14.1 1.3 %collective-permute-start.3 = (f32[2,8,4,256]{3,2,1,0:T(4,128)S(1)}, f32[2,8,4,256]{3,2,1,0:T(4,128)S(1)}, u32[]{:S(2)}, u32[]{:S(2)}) collective-permute-start(f32[2,8,4,256]{3,2,1,0:T(4,128)S(1)} %get-tuple-element.42), channel_id=1, source_target_pairs={{8,0},{16,8},{24,16},{9,1},{17,9},{25,17},{10,2},{18,10},{26,18},{... | collective-permute-start | bytes 196616 | tf_op jit(solution)/shard_map/ppermute | solution.py:21
  15.4 0.6 collective-permute-done.2
  16.0 4.4 %collective-permute-done.3 = f32[2,8,4,256]{3,2,1,0:T(4,128)S(1)} collective-permute-done((f32[2,8,4,256]{3,2,1,0:T(4,128)S(1)}, f32[2,8,4,256]{3,2,1,0:T(4,128)S(1)}, u32[]{:S(2)}, u32[]{:S(2)}) %collective-permute-start.3) | collective-permute-done | bytes 65568 | tf_op jit(solution)/shard_map/ppermute | solution.py:21
  20.5 0.1 copy.141
  21.9 0.1 pad_maximum_fusion.6
  22.0 0.4 copy.165
  22.7 0.1 multiply_bitcast_fusion.1
  22.8 0.2 copy.175
  23.0 0.2 copy.174
  23.2 0.1 pad_maximum_fusion.4
  23.4 0.4 copy.142
  24.1 0.1 multiply_bitcast_fusion.3
  24.2 0.2 copy.171
  24.4 0.6 %constant_dynamic-update-slice_fusion.13 = f32[7,8,8,128]{3,2,1,0:T(8,128)} fusion(f32[1,8,8,128]{3,2,1,0:T(8,128)S(1)} %copy.171), kind=kLoop, calls=%fused_computation.156 | loop fusion | bytes 65536
  25.0 1.0 %fusion.127 = (f32[8,4,128]{1,0,2:T(8,128)}, f32[8,4,128]{1,0,2:T(8,128)S(1)}) fusion(f32[8,8,128]{1,0,2:T(8,128)S(1)} %get-tuple-element.27), kind=kLoop, calls=%fused_computation.244 | loop fusion | bytes 65536 | tf_op jit(solution)/shard_map/slice | solution.py:18
  26.0 3.5 %collective-permute-start.4 = (f32[8,4,128]{1,0,2:T(8,128)}, f32[8,4,128]{1,0,2:T(8,128)S(1)}, u32[]{:S(2)}, u32[]{:S(2)}) collective-permute-start(f32[8,4,128]{1,0,2:T(8,128)} %get-tuple-element.28), channel_id=1, source_target_pairs={{0,8},{8,16},{16,24},{1,9},{9,17},{17,25},{2,10},{10,18},{18,26},{... | collective-permute-start | bytes 49160 | tf_op jit(solution)/shard_map/ppermute | solution.py:20
  29.5 1.3 %collective-permute-start.5 = (f32[8,4,128]{1,0,2:T(8,128)S(1)}, f32[8,4,128]{1,0,2:T(8,128)S(1)}, u32[]{:S(2)}, u32[]{:S(2)}) collective-permute-start(f32[8,4,128]{1,0,2:T(8,128)S(1)} %get-tuple-element.29), channel_id=1, source_target_pairs={{8,0},{16,8},{24,16},{9,1},{17,9},{25,17},{10,2},{18,10},{26,18},{... | collective-permute-start | bytes 49160 | tf_op jit(solution)/shard_map/ppermute | solution.py:21
  30.9 0.4 copy.162
  31.7 0.1 multiply_bitcast_fusion.2
  31.8 0.2 copy.173
  32.0 0.2 copy.172
  32.2 0.1 pad_maximum_fusion.7
  32.3 0.4 copy.168
  33.1 0.1 multiply_bitcast_fusion
  33.2 0.2 copy.176
  33.4 0.6 %constant_dynamic-update-slice_fusion.12 = f32[7,8,8,128]{3,2,1,0:T(8,128)} fusion(f32[7,8,8,128]{3,2,1,0:T(8,128)} %constant_dynamic-update-slice_fusion.13, f32[1,8,8,128]{3,2,1,0:T(8,128)S(1)} %copy.172), kind=kLoop, calls=%fused_computation.155 | loop fusion | bytes 65536
  34.0 0.6 constant_dynamic-update-slice_fusion.11
  34.6 0.6 constant_dynamic-update-slice_fusion.10
  35.3 0.6 constant_dynamic-update-slice_fusion.9
  35.9 0.6 constant_dynamic-update-slice_fusion.8
  36.5 0.2 copy.145
  36.7 0.2 copy.177
  36.9 4.0 %collective-permute-done.4 = f32[8,4,128]{1,0,2:T(8,128)S(1)} collective-permute-done((f32[8,4,128]{1,0,2:T(8,128)}, f32[8,4,128]{1,0,2:T(8,128)S(1)}, u32[]{:S(2)}, u32[]{:S(2)}) %collective-permute-start.4) | collective-permute-done | bytes 16416 | tf_op jit(solution)/shard_map/ppermute | solution.py:20
  40.8 0.2 copy.144
  41.0 3.6 %collective-permute-done.5 = f32[8,4,128]{1,0,2:T(8,128)S(1)} collective-permute-done((f32[8,4,128]{1,0,2:T(8,128)S(1)}, f32[8,4,128]{1,0,2:T(8,128)S(1)}, u32[]{:S(2)}, u32[]{:S(2)}) %collective-permute-start.5) | collective-permute-done | bytes 16416 | tf_op jit(solution)/shard_map/ppermute | solution.py:21
  44.7 0.2 copy.146
  44.9 3.3 %collective-permute-start.7 = (f32[4,16,128]{2,1,0:T(8,128)S(1)}, f32[4,16,128]{2,1,0:T(8,128)S(1)}, u32[]{:S(2)}, u32[]{:S(2)}) collective-permute-start(f32[4,16,128]{2,1,0:T(8,128)S(1)} %get-tuple-element.65), channel_id=1, source_target_pairs={{1,0},{2,1},{3,2},{4,3},{5,4},{6,5},{7,6},{9,8},{10,9},{11,10},{12... | collective-permute-start | bytes 98312 | tf_op jit(solution)/shard_map/ppermute | solution.py:21
  48.2 0.6 constant_dynamic-update-slice_fusion.7
  48.8 1.9 %collective-permute-start.6 = (f32[4,16,128]{2,1,0:T(8,128)S(1)}, f32[4,16,128]{2,1,0:T(8,128)S(1)}, u32[]{:S(2)}, u32[]{:S(2)}) collective-permute-start(f32[4,16,128]{2,1,0:T(8,128)S(1)} %get-tuple-element.67), channel_id=1, source_target_pairs={{0,1},{1,2},{2,3},{3,4},{4,5},{5,6},{6,7},{8,9},{9,10},{10,11},{11... | collective-permute-start | bytes 98312 | tf_op jit(solution)/shard_map/ppermute | solution.py:20
  50.8 4.2 %collective-permute-done.6 = f32[4,16,128]{2,1,0:T(8,128)S(1)} collective-permute-done((f32[4,16,128]{2,1,0:T(8,128)S(1)}, f32[4,16,128]{2,1,0:T(8,128)S(1)}, u32[]{:S(2)}, u32[]{:S(2)}) %collective-permute-start.6) | collective-permute-done | bytes 32800 | tf_op jit(solution)/shard_map/ppermute | solution.py:20
  55.7 0.2 copy.148
  55.9 0.2 fusion.131
  56.1 0.1 copy.150
  56.2 0.1 copy.149
  56.6 0.7 %fusion.117 = f32[4,4,64]{2,1,0:T(4,128)} fusion(f32[4,4,65]{2,1,0:T(4,128)S(1)} %fusion.119, f32[4,4,66]{2,1,0:T(4,128)S(1)} %fusion.121), kind=kLoop, calls=%fused_computation.228 | loop fusion | flops 4096 | bytes 16384 | tf_op jit(solution)/shard_map/mul | solution.py:52
  58.3 0.2 copy.151
  58.5 0.2 fusion.130
  58.7 0.1 copy.181
  58.9 0.1 copy.180
  59.5 0.2 copy.156
  59.6 0.2 fusion.129
  60.0 0.1 copy.184
  60.6 0.2 copy.159
  60.8 0.2 fusion.128
  61.0 0.1 copy.187
  61.1 0.1 copy.186
  61.6 0.6 %copy-done.1 = f32[7,4,4,64]{3,2,1,0:T(4,128)} copy-done((f32[7,4,4,64]{3,2,1,0:T(4,128)}, f32[7,4,4,64]{3,2,1,0:T(4,128)S(1)}, u32[]{:S(2)}) %copy-start.1) | copy-done | bytes 28696
  (113 shorter events, 6.2 us)
Async XLA Ops:
  0.6 9.4 %copy-start = (f32[16,16,256]{2,1,0:T(8,128)S(1)}, f32[16,16,256]{2,1,0:T(8,128)}, u32[]{:S(2)}) copy-start(f32[16,16,256]{2,1,0:T(8,128)} %param.1) | copy-start | bytes 786436
  1.6 6.5 %collective-permute-start = (f32[4,16,256]{2,1,0:T(8,128)S(1)}, f32[4,16,256]{2,1,0:T(8,128)S(1)}, u32[]{:S(2)}, u32[]{:S(2)}) collective-permute-start(f32[4,16,256]{2,1,0:T(8,128)S(1)} %get-tuple-element.46), channel_id=1, source_target_pairs={{0,1},{1,2},{2,3},{3,4},{4,5},{5,6},{6,7},{8,9},{9,10},{10,11},{11... | collective-permute-start | bytes 196616 | tf_op jit(solution)/shard_map/ppermute | solution.py:20
  3.6 6.4 %collective-permute-start.1 = (f32[4,16,256]{2,1,0:T(8,128)S(1)}, f32[4,16,256]{2,1,0:T(8,128)S(1)}, u32[]{:S(2)}, u32[]{:S(2)}) collective-permute-start(f32[4,16,256]{2,1,0:T(8,128)S(1)} %get-tuple-element.47), channel_id=1, source_target_pairs={{1,0},{2,1},{3,2},{4,3},{5,4},{6,5},{7,6},{9,8},{10,9},{11,10},{12... | collective-permute-start | bytes 196616 | tf_op jit(solution)/shard_map/ppermute | solution.py:21
  10.3 5.7 %collective-permute-start.2 = (f32[2,8,4,256]{3,2,1,0:T(4,128)S(1)}, f32[2,8,4,256]{3,2,1,0:T(4,128)S(1)}, u32[]{:S(2)}, u32[]{:S(2)}) collective-permute-start(f32[2,8,4,256]{3,2,1,0:T(4,128)S(1)} %get-tuple-element.40), channel_id=1, source_target_pairs={{0,8},{8,16},{16,24},{1,9},{9,17},{17,25},{2,10},{10,18},{18,26},{... | collective-permute-start | bytes 196616 | tf_op jit(solution)/shard_map/ppermute | solution.py:20
  14.1 6.4 %collective-permute-start.3 = (f32[2,8,4,256]{3,2,1,0:T(4,128)S(1)}, f32[2,8,4,256]{3,2,1,0:T(4,128)S(1)}, u32[]{:S(2)}, u32[]{:S(2)}) collective-permute-start(f32[2,8,4,256]{3,2,1,0:T(4,128)S(1)} %get-tuple-element.42), channel_id=1, source_target_pairs={{8,0},{16,8},{24,16},{9,1},{17,9},{25,17},{10,2},{18,10},{26,18},{... | collective-permute-start | bytes 196616 | tf_op jit(solution)/shard_map/ppermute | solution.py:21
  26.0 14.8 %collective-permute-start.4 = (f32[8,4,128]{1,0,2:T(8,128)}, f32[8,4,128]{1,0,2:T(8,128)S(1)}, u32[]{:S(2)}, u32[]{:S(2)}) collective-permute-start(f32[8,4,128]{1,0,2:T(8,128)} %get-tuple-element.28), channel_id=1, source_target_pairs={{0,8},{8,16},{16,24},{1,9},{9,17},{17,25},{2,10},{10,18},{18,26},{... | collective-permute-start | bytes 49160 | tf_op jit(solution)/shard_map/ppermute | solution.py:20
  29.5 15.1 %collective-permute-start.5 = (f32[8,4,128]{1,0,2:T(8,128)S(1)}, f32[8,4,128]{1,0,2:T(8,128)S(1)}, u32[]{:S(2)}, u32[]{:S(2)}) collective-permute-start(f32[8,4,128]{1,0,2:T(8,128)S(1)} %get-tuple-element.29), channel_id=1, source_target_pairs={{8,0},{16,8},{24,16},{9,1},{17,9},{25,17},{10,2},{18,10},{26,18},{... | collective-permute-start | bytes 49160 | tf_op jit(solution)/shard_map/ppermute | solution.py:21
  44.9 5.8 %collective-permute-start.7 = (f32[4,16,128]{2,1,0:T(8,128)S(1)}, f32[4,16,128]{2,1,0:T(8,128)S(1)}, u32[]{:S(2)}, u32[]{:S(2)}) collective-permute-start(f32[4,16,128]{2,1,0:T(8,128)S(1)} %get-tuple-element.65), channel_id=1, source_target_pairs={{1,0},{2,1},{3,2},{4,3},{5,4},{6,5},{7,6},{9,8},{10,9},{11,10},{12... | collective-permute-start | bytes 98312 | tf_op jit(solution)/shard_map/ppermute | solution.py:21
  48.8 6.1 %collective-permute-start.6 = (f32[4,16,128]{2,1,0:T(8,128)S(1)}, f32[4,16,128]{2,1,0:T(8,128)S(1)}, u32[]{:S(2)}, u32[]{:S(2)}) collective-permute-start(f32[4,16,128]{2,1,0:T(8,128)S(1)} %get-tuple-element.67), channel_id=1, source_target_pairs={{0,1},{1,2},{2,3},{3,4},{4,5},{5,6},{6,7},{8,9},{9,10},{10,11},{11... | collective-permute-start | bytes 98312 | tf_op jit(solution)/shard_map/ppermute | solution.py:20
  61.6 0.6 %copy-start.1 = (f32[7,4,4,64]{3,2,1,0:T(4,128)}, f32[7,4,4,64]{3,2,1,0:T(4,128)S(1)}, u32[]{:S(2)}) copy-start(f32[7,4,4,64]{3,2,1,0:T(4,128)S(1)} %constant_dynamic-update-slice_fusion) | copy-start | bytes 86020
where the time goes:
time: 62.6 us; the launch traced here: 62.3 us
  starting transfers between devices  21.2 us (34%)
  waiting for transfers between devices  18.7 us (30%)
  local copies, waits for them, and re-layouts  16 us (26%)
  other arithmetic  5.05 us (8%)
  between operations  1.34 us (2%)
    ppermute x4, starting transfers between devices, extended_2(): before = lax.ppermute(last, axis, up)  10.8 us
    ppermute x4, starting transfers between devices, extended_2(): after = lax.ppermute(initial, axis, down)  10.4 us
    ppermute x4, waiting for transfers between devices, extended_2(): after = lax.ppermute(initial, axis, down)  9.9 us
    ppermute x4, waiting for transfers between devices, extended_2(): before = lax.ppermute(last, axis, up)  8.75 us
    unnamed x16, local copies, waits for them, and re-layouts  5.02 us
    concatenate x8, local copies, waits for them, and re-layouts, split_depth(): padded = jnp.pad(x_band, ((0, 0), (0, 0), (4, 4)), mode='reflect')  2.39 us
    another operation x8, local copies, waits for them, and re-layouts, per_device(): detail_one = jnp.stack([subband for subband in level_one[1:]])  1.97 us
    rev x16, local copies, waits for them, and re-layouts, split_depth(): padded = jnp.pad(x_band, ((0, 0), (0, 0), (4, 4)), mode='reflect')  1.4 us
  transfers between devices with their start and end apart: 8, of which 6 were waited for; matrix products, arithmetic and copies ran while one was open for 11% of the time, Pallas kernels for 0%

commit v1 on v0

v1 whole, which is shorter than its diff:
```python
import functools

import jax
import jax.numpy as jnp
import numpy as np
from jax import lax
from jax.experimental import pallas as pl
from jax.experimental.pallas import tpu as pltpu
from jax.sharding import PartitionSpec as P

LIFT_ALPHA = -1.586134342059924
LIFT_BETA = -0.052980118572961
LIFT_GAMMA = 0.882911075530934
LIFT_DELTA = 0.443506852043971
LIFT_SCALE = 1.149604398860241

MESH = pl.DeviceIdType.MESH
FACES = ((1, 0), (-1, 0), (0, 1), (0, -1))
CORNERS = ((1, 1), (1, -1), (-1, 1), (-1, -1))
WAYS = FACES + CORNERS
HIGHEST = lax.Precision.HIGHEST


def lift_matrix(n):
    x = np.pad(np.eye(n), ((4, 4), (0, 0)), mode="reflect")
    e, o = x[0::2], x[1::2]
    d1 = o[:-1] + LIFT_ALPHA * (e[:-1] + e[1:])
    s1 = e[1:-1] + LIFT_BETA * (d1[:-1] + d1[1:])
    d2 = d1[1:-1] + LIFT_GAMMA * (s1[:-1] + s1[1:])
    s2 = s1[1:-1] + LIFT_DELTA * (d2[:-1] + d2[1:])
    return s2 * LIFT_SCALE, d2[1:] / LIFT_SCALE


def low_rank(coupling, rank):
    rest, us, vs = coupling.copy(), [], []
    for _ in range(rank):
        i, j = np.unravel_index(np.argmax(np.abs(rest)), rest.shape)
        u, v = rest[:, j] / rest[i, j], rest[i, :].copy()
        us.append(u)
        vs.append(v)
        rest = rest - u[:, None] * v[None, :]
    assert np.abs(rest).max() < 1e-12
    return np.stack(us, 1), np.stack(vs, 0)


def block_maps(b):
    blocks = 5
    low, high = lift_matrix(blocks * b)
    low2, high2 = lift_matrix(blocks * b // 2)
    pairs = ((low, high, 2), (low2 @ low, high2 @ low, 4))
    levels = []
    for lows, highs, rank in pairs:
        n = lows.shape[0] // blocks

        def part(row, col):
            cols = slice(col * b, (col + 1) * b)
            rows = slice(row * n, (row + 1) * n)
            return np.concatenate([lows[rows, cols], highs[rows, cols]])

        for row in range(blocks):
            for col in range(blocks):
                if abs(row - col) > 1:
                    assert np.abs(part(row, col)).max() == 0
                elif row != col:
                    like = part(2, 2 + col - row)
                    assert np.abs(part(row, col) - like).max() < 1e-12
        assert np.abs(part(1, 1) - part(2, 2)).max() < 1e-12
        assert np.abs(part(3, 3) - part(2, 2)).max() < 1e-12
        own = [part(0, 0), part(2, 2), part(4, 4)]
        u_up, v_up = low_rank(part(2, 1), rank)
        u_down, v_down = low_rank(part(2, 3), rank)
        levels.append((own, {1: u_up, -1: u_down}, {1: v_up, -1: v_down}))
    return levels


@functools.lru_cache(maxsize=None)
def matrices(bx, by, nz):
    low, high = lift_matrix(nz)
    low2, high2 = lift_matrix(nz // 2)
    depth = np.concatenate([low, high, low2 @ low, high2 @ low]).T
    sends, spreads = [], []
    for level, pad in ((0, 1), (1, 2)):
        own_x, ux, vx = block_maps(bx)[level]
        own_y, uy, vy = block_maps(by)[level]
        nx, ny = own_x[0].shape[0], own_y[0].shape[0]
        eye_x, eye_y = np.eye(nx), np.eye(ny)
        spread = [np.kron(ux[dx] if dx else eye_x, uy[dy] if dy else eye_y) for dx, dy in WAYS]

        def by_band(m):
            m = m.reshape(2, nx // 2, 2, ny // 2, -1).transpose(0, 2, 1, 3, 4)
            m = np.pad(m, ((0, 0),) * 3 + ((0, (pad - 1) * (ny // 2)), (0, 0)))
            return m.reshape(-1, m.shape[-1])

        spreads.append(by_band(np.concatenate(spread, 1)).astype(np.float32))
        rows = []
        for cx in range(3):
            for cy in range(3):
                out = [
                    np.kron(vx[dx] if dx else own_x[cx], vy[dy] if dy else own_y[cy])
                    for dx, dy in WAYS
                ]
                out.append(by_band(np.kron(own_x[cx], own_y[cy])))
                rows.append(np.concatenate(out))
        sends.append(np.stack(rows).astype(np.float32))
    return depth.astype(np.float32), sends[0], sends[1], spreads[0], spreads[1]


FACE, CORNER = 96, 24
SLOTS = tuple((k * FACE, FACE) for k in range(4)) + tuple(
    (4 * FACE + k * CORNER, CORNER) for k in range(4)
)


def dot(a, b):
    return jnp.dot(a, b, precision=HIGHEST, preferred_element_type=jnp.float32)


def kernel(
    nx, ny, x_hbm, t_hbm, s1_hbm, s2_hbm, u1_hbm, u2_hbm, approx, two, one,
    x_v, t_v, s1_v, s2_v, u1_v, u2_v, out_buf, in_buf, load_sem, send_sem, recv_sem,
):
    px, py = lax.axis_index("slab"), lax.axis_index("morton")
    not_first_x, last_x = lax.div(px + (nx - 2), nx - 1), lax.div(px, nx - 1)
    not_first_y, last_y = lax.div(py + (ny - 2), ny - 1), lax.div(py, ny - 1)
    here = (not_first_x + last_x) * 3 + not_first_y + last_y
    has_x = {1: 1 - last_x, -1: not_first_x, 0: 1}
    has_y = {1: 1 - last_y, -1: not_first_y, 0: 1}

    def exists(dx, dy):
        return has_x[dx] * has_y[dy] == 1

    loads = [
        pltpu.make_async_copy(source, target, load_sem.at[k])
        for k, (source, target) in enumerate((
            (x_hbm, x_v), (t_hbm, t_v), (s1_hbm.at[here], s1_v),
            (s2_hbm.at[here], s2_v), (u1_hbm, u1_v), (u2_hbm, u2_v),
        ))
    ]
    for load in loads:
        load.start()

    barrier = pltpu.get_barrier_semaphore()
    for dx, dy in WAYS:
        @pl.when(exists(dx, dy))
        def _():
            pl.semaphore_signal(
                barrier, inc=1, device_id=(py + dy, px + dx), device_id_type=MESH
            )

    for (dx, dy), (start, size) in zip(WAYS, SLOTS):
        @pl.when(jnp.logical_not(exists(-dx, -dy)))
        def _():
            in_buf[start:start + size, :] = jnp.zeros((size, 128), jnp.float32)

    loads[0].wait()
    loads[1].wait()
    z = dot(x_v[...].reshape(256, 256), t_v[...])
    z1, z2 = z[:, :256], z[:, 256:]
    loads[2].wait()
    p1 = dot(s1_v[:144, :], z1)
    loads[3].wait()
    p2 = dot(s2_v[:192, :], z2)
    for k in range(4):
        at = k * FACE
        out_buf[at:at + 32, :] = p1[k * 32:k * 32 + 32, :128]
        out_buf[at + 32:at + 64, :] = p1[k * 32:k * 32 + 32, 128:]
        out_buf[at + 64:at + 96, :] = p2[k * 32:k * 32 + 32, :]
        at = 4 * FACE + k * CORNER
        out_buf[at:at + 4, :] = p1[128 + k * 4:132 + k * 4, :128]
        out_buf[at + 4:at + 8, :] = p1[128 + k * 4:132 + k * 4, 128:]
        out_buf[at + 8:at + 24, :] = p2[128 + k * 16:144 + k * 16, :]

    pl.semaphore_wait(
        barrier,
        (1 + has_x[1] + has_x[-1]) * (1 + has_y[1] + has_y[-1]) - 1,
    )

    def message(k):
        (dx, dy), (start, size) = WAYS[k], SLOTS[k]
        return pltpu.make_async_remote_copy(
            src_ref=out_buf.at[pl.ds(start, size)],
            dst_ref=in_buf.at[pl.ds(start, size)],
            send_sem=send_sem.at[k],
            recv_sem=recv_sem.at[k],
            device_id=(py + dy, px + dx),
            device_id_type=MESH,
        )

    order = (2, 3, 4, 5, 6, 7, 0, 1)
    for k in order:
        @pl.when(exists(*WAYS[k]))
        def _():
            message(k).start()

    own1 = dot(s1_v[144:, :], z1)
    own2 = dot(s2_v[192:, :], z2)
    loads[4].wait()
    loads[5].wait()

    for k in order:
        dx, dy = WAYS[k]

        @pl.when(exists(-dx, -dy))
        def _():
            message(k).wait_recv()

    halo1 = [
        jnp.concatenate(
            [in_buf[k * FACE:k * FACE + 32, :], in_buf[k * FACE + 32:k * FACE + 64, :]], axis=1
        )
        for k in range(4)
    ]
    halo2 = [in_buf[k * FACE + 64:k * FACE + 96, :] for k in range(4)]
    for k in range(4):
        at = 4 * FACE + k * CORNER
        halo1.append(jnp.concatenate([in_buf[at:at + 4, :], in_buf[at + 4:at + 8, :]], axis=1))
        halo2.append(in_buf[at + 8:at + 24, :])
    o2 = own2 + dot(u2_v[...], jnp.concatenate(halo2, axis=0))
    o1 = own1 + dot(u1_v[...], jnp.concatenate(halo1, axis=0))

    o2 = o2.reshape(4, 4, 8, 128)
    for band in range(4):
        for bz in range(2):
            part = o2[band, :, :4, bz * 64:bz * 64 + 64]
            if band + bz:
                two[2 * band + bz - 1] = part
                one[2 * band + bz - 1] = o1[
                    band * 64:band * 64 + 64, bz * 128:bz * 128 + 128
                ].reshape(8, 8, 128)
            else:
                approx[...] = part

    for k in order:
        @pl.when(exists(*WAYS[k]))
        def _():
            message(k).wait_send()


def per_device(nx, ny, velocity):
    bx, by, nz = velocity.shape
    consts = matrices(bx, by, nz)
    f32 = jnp.float32
    vmem = pl.BlockSpec(memory_space=pltpu.VMEM)
    tables = [pltpu.VMEM(c.shape[-2:], f32) for c in consts]
    return pl.pallas_call(
        functools.partial(kernel, nx, ny),
        out_shape=(
            jax.ShapeDtypeStruct((bx // 4, by // 4, nz // 4), f32),
            jax.ShapeDtypeStruct((7, bx // 4, by // 4, nz // 4), f32),
            jax.ShapeDtypeStruct((7, bx // 2, by // 2, nz // 2), f32),
        ),
        in_specs=[pl.BlockSpec(memory_space=pl.ANY)] * 6,
        out_specs=(vmem, vmem, vmem),
        scratch_shapes=[pltpu.VMEM((bx, by, nz), f32)]
        + tables
        + [
            pltpu.VMEM((4 * (FACE + CORNER), 128), f32),
            pltpu.VMEM((4 * (FACE + CORNER), 128), f32),
            pltpu.SemaphoreType.DMA((6,)),
            pltpu.SemaphoreType.DMA((8,)),
            pltpu.SemaphoreType.DMA((8,)),
        ],
        compiler_params=pltpu.CompilerParams(
            collective_id=0, has_side_effects=True, vmem_limit_bytes=60 * 1024 * 1024
        ),
    )(velocity, *[jnp.asarray(c) for c in consts])


def solution(mesh):
    placed = (P("slab", "morton", None),)
    return jax.shard_map(
        functools.partial(per_device, mesh.shape["slab"], mesh.shape["morton"]),
        mesh=mesh,
        in_specs=placed,
        out_specs=(
            P("slab", "morton", None),
            P(None, "slab", "morton", None),
            P(None, "slab", "morton", None),
        ),
        check_vma=False,
    )
```

time: 62.6 us -> 15.8 us (0.25)
  the two profiles are of different devices: /device:TPU:4 before, /device:TPU:1 now
where the time goes in v1:
time: 15.8 us; the launch traced here: 15.6 us
  Pallas kernels  10.5 us (66%)
  local copies, waits for them, and re-layouts  4.38 us (28%)
  between operations  0.64 us (4%)
    pallas_call x1, Pallas kernels, per_device(): pl.pallas_call(functools.partial(kernel, nx, ny), out_shape=(jax.ShapeDty...  10.5 us
    unnamed x3, local copies, waits for them, and re-layouts  4.38 us

profile of v1, /device:TPU:1, one launch (start us, length us, event | category | flops | bytes accessed | tf_op | source)
XLA Modules:
  0.0 15.6 jit_solution(16789485328656121416)
XLA Ops:
  0.6 10.5 %shard_map.85 = (f32[4,4,64]{2,1,0:T(4,128)}, f32[7,4,4,64]{3,2,1,0:T(4,128)}, f32[7,8,8,128]{3,2,1,0:T(8,128)}) custom-call(f32[16,16,256]{2,1,0:T(8,128)} %x_hbm.1, f32[256,384]{1,0:T(8,128)} %constant.10.clone.t_hbm, f32[9,400,256]{2,1,0:T(8,128)} %constant.11.clone.s1_hbm, f32[9,320,256]{2,1,0:T(8,128)} %constant.12.clone.s2_hbm, ...), custom_call_target="tpu_custom_call" | custom-call | tf_op jit(solution)/shard_map/pallas_call | solution.py:245
  11.2 1.3 %copy.12 = f32[4,4,64]{2,1,0:T(4,128)} copy(f32[4,4,64]{2,1,0:T(4,128)} %get-tuple-element.6) | data formatting | bytes 8192
  12.5 1.4 %copy.13 = f32[7,4,4,64]{3,2,1,0:T(4,128)} copy(f32[7,4,4,64]{3,2,1,0:T(4,128)} %get-tuple-element.7) | data formatting | bytes 57344
  13.9 1.6 %copy.14 = f32[7,8,8,128]{3,2,1,0:T(8,128)} copy(f32[7,8,8,128]{3,2,1,0:T(8,128)} %get-tuple-element.8) | data formatting | bytes 458752

commit v2 on v1

--- a/solution.py
+++ b/solution.py
@@ -236,19 +236,29 @@
             message(k).wait_send()
 
 
+def store(approx_v, two_v, one_v, approx, two, one, sem):
+    pairs = ((one_v, one), (two_v, two), (approx_v, approx))
+    copies = [pltpu.make_async_copy(a, b, sem.at[k]) for k, (a, b) in enumerate(pairs)]
+    for copy in copies:
+        copy.start()
+    for copy in copies:
+        copy.wait()
+
+
 def per_device(nx, ny, velocity):
     bx, by, nz = velocity.shape
     consts = matrices(bx, by, nz)
     f32 = jnp.float32
     vmem = pl.BlockSpec(memory_space=pltpu.VMEM)
     tables = [pltpu.VMEM(c.shape[-2:], f32) for c in consts]
-    return pl.pallas_call(
+    shapes = (
+        (bx // 4, by // 4, nz // 4),
+        (7, bx // 4, by // 4, nz // 4),
+        (7, bx // 2, by // 2, nz // 2),
+    )
+    results = pl.pallas_call(
         functools.partial(kernel, nx, ny),
-        out_shape=(
-            jax.ShapeDtypeStruct((bx // 4, by // 4, nz // 4), f32),
-            jax.ShapeDtypeStruct((7, bx // 4, by // 4, nz // 4), f32),
-            jax.ShapeDtypeStruct((7, bx // 2, by // 2, nz // 2), f32),
-        ),
+        out_shape=tuple(pltpu.VMEM(shape, f32) for shape in shapes),
         in_specs=[pl.BlockSpec(memory_space=pl.ANY)] * 6,
         out_specs=(vmem, vmem, vmem),
         scratch_shapes=[pltpu.VMEM((bx, by, nz), f32)]
@@ -264,6 +274,14 @@
             collective_id=0, has_side_effects=True, vmem_limit_bytes=60 * 1024 * 1024
         ),
     )(velocity, *[jnp.asarray(c) for c in consts])
+    results = [pltpu.with_memory_space_constraint(r, pltpu.VMEM) for r in results]
+    return pl.pallas_call(
+        store,
+        out_shape=tuple(jax.ShapeDtypeStruct(shape, f32) for shape in shapes),
+        in_specs=[vmem] * 3,
+        out_specs=[pl.BlockSpec(memory_space=pl.ANY)] * 3,
+        scratch_shapes=[pltpu.SemaphoreType.DMA((3,))],
+    )(*results)
 
 
 def solution(mesh):

time: 15.8 us -> 11.4 us (0.72)
  local copies, waits for them, and re-layouts: 4.38 us -> 0 us
    unnamed x3 -> x0, local copies, waits for them, and re-layouts: 4.38 us -> none
    pallas_call x1 -> x2, Pallas kernels: 10.5 us -> 10.6 us  [the longest x1 9.84 us: per_device(): pl.pallas_call(functools.partial(kernel, nx, ny), out_shape=tuple((pltpu....]
where the time goes in v2:
time: 11.4 us; the launch traced here: 11.2 us
  Pallas kernels  10.6 us (93%)
  between operations  0.64 us (6%)
    pallas_call x1, Pallas kernels, per_device(): pl.pallas_call(functools.partial(kernel, nx, ny), out_shape=tuple((pltpu....  9.84 us
    pallas_call x1, Pallas kernels, per_device(): pl.pallas_call(store, out_shape=tuple((jax.ShapeDtypeStruct(shape, f32) f...  0.73 us

profile of v2, /device:TPU:1, one launch (start us, length us, event | category | flops | bytes accessed | tf_op | source)
XLA Modules:
  0.0 11.2 jit_solution(1156006206354906306)
XLA Ops:
  0.6 9.8 %shard_map.85 = (f32[4,4,64]{2,1,0:T(4,128)S(1)}, f32[7,4,4,64]{3,2,1,0:T(4,128)S(1)}, f32[7,8,8,128]{3,2,1,0:T(8,128)S(1)}) custom-call(f32[16,16,256]{2,1,0:T(8,128)} %x_hbm.1, f32[256,384]{1,0:T(8,128)} %constant.10.clone.t_hbm, f32[9,400,256]{2,1,0:T(8,128)} %constant.11.clone.s1_hbm, f32[9,320,256]{2,1,0:T(8,128)} %constant.12.clone.s2_hbm, ...), custom_call_target="tpu_custom_call" | custom-call | tf_op jit(solution)/shard_map/pallas_call | solution.py:259
  10.5 0.7 %shard_map.86 = (f32[4,4,64]{2,1,0:T(4,128)}, f32[7,4,4,64]{3,2,1,0:T(4,128)}, f32[7,8,8,128]{3,2,1,0:T(8,128)}) custom-call(f32[4,4,64]{2,1,0:T(4,128)S(1)} %get-tuple-element.6.approx_v, f32[7,4,4,64]{3,2,1,0:T(4,128)S(1)} %get-tuple-element.7.two_v, f32[7,8,8,128]{3,2,1,0:T(8,128)S(1)} %get-tuple-element.8.one_v), custom_call_target="tpu_custom_call" | custom-call | tf_op jit(solution)/shard_map/pallas_call | solution.py:278

commit v3 on v2

--- a/solution.py
+++ b/solution.py
@@ -18,6 +18,7 @@
 FACES = ((1, 0), (-1, 0), (0, 1), (0, -1))
 CORNERS = ((1, 1), (1, -1), (-1, 1), (-1, -1))
 WAYS = FACES + CORNERS
+ORDER = (2, 3, 4, 5, 6, 7, 0, 1)
 HIGHEST = lax.Precision.HIGHEST
 
 
@@ -77,7 +78,8 @@
 def matrices(bx, by, nz):
     low, high = lift_matrix(nz)
     low2, high2 = lift_matrix(nz // 2)
-    depth = np.concatenate([low, high, low2 @ low, high2 @ low]).T
+    depth1 = np.concatenate([low, high]).T.astype(np.float32)
+    depth2 = np.concatenate([low2 @ low, high2 @ low]).T.astype(np.float32)
     sends, spreads = [], []
     for level, pad in ((0, 1), (1, 2)):
         own_x, ux, vx = block_maps(bx)[level]
@@ -102,13 +104,7 @@
                 out.append(by_band(np.kron(own_x[cx], own_y[cy])))
                 rows.append(np.concatenate(out))
         sends.append(np.stack(rows).astype(np.float32))
-    return depth.astype(np.float32), sends[0], sends[1], spreads[0], spreads[1]
-
-
-FACE, CORNER = 96, 24
-SLOTS = tuple((k * FACE, FACE) for k in range(4)) + tuple(
-    (4 * FACE + k * CORNER, CORNER) for k in range(4)
-)
+    return depth1, depth2, sends[0], sends[1], spreads[0], spreads[1]
 
 
 def dot(a, b):
@@ -116,8 +112,10 @@
 
 
 def kernel(
-    nx, ny, x_hbm, t_hbm, s1_hbm, s2_hbm, u1_hbm, u2_hbm, approx, two, one,
-    x_v, t_v, s1_v, s2_v, u1_v, u2_v, out_buf, in_buf, load_sem, send_sem, recv_sem,
+    nx, ny, x_hbm, t1_hbm, t2_hbm, s1_hbm, s2_hbm, u1_hbm, u2_hbm, approx, two, one,
+    x_v, t1_v, t2_v, s1_v, s2_v, u1_v, u2_v,
+    face1_out, face1_in, corner1_out, corner1_in, out2, in2,
+    load_sem, send1, recv1, send2, recv2,
 ):
     px, py = lax.axis_index("slab"), lax.axis_index("morton")
     not_first_x, last_x = lax.div(px + (nx - 2), nx - 1), lax.div(px, nx - 1)
@@ -129,11 +127,22 @@
     def exists(dx, dy):
         return has_x[dx] * has_y[dy] == 1
 
+    def rows(ref, start, size):
+        return ref.at[pl.ds(start, size)]
+
+    n1, n2 = s1_v.shape[0] - 144, s2_v.shape[0] - 192
     loads = [
         pltpu.make_async_copy(source, target, load_sem.at[k])
         for k, (source, target) in enumerate((
-            (x_hbm, x_v), (t_hbm, t_v), (s1_hbm.at[here], s1_v),
-            (s2_hbm.at[here], s2_v), (u1_hbm, u1_v), (u2_hbm, u2_v),
+            (x_hbm, x_v),
+            (t1_hbm, t1_v),
+            (s1_hbm.at[here, pl.ds(0, 144)], rows(s1_v, 0, 144)),
+            (t2_hbm, t2_v),
+            (s2_hbm.at[here, pl.ds(0, 192)], rows(s2_v, 0, 192)),
+            (s1_hbm.at[here, pl.ds(144, n1)], rows(s1_v, 144, n1)),
+            (s2_hbm.at[here, pl.ds(192, n2)], rows(s2_v, 192, n2)),
+            (u1_hbm, u1_v),
+            (u2_hbm, u2_v),
         ))
     ]
     for load in loads:
@@ -147,93 +156,100 @@
                 barrier, inc=1, device_id=(py + dy, px + dx), device_id_type=MESH
             )
 
-    for (dx, dy), (start, size) in zip(WAYS, SLOTS):
+    def message(level, k):
+        dx, dy = WAYS[k]
+        if level == 1 and k < 4:
+            pair = rows(face1_out, k * 32, 32), rows(face1_in, k * 32, 32)
+        elif level == 1:
+            pair = corner1_out.at[k - 4], corner1_in.at[k - 4]
+        elif k < 4:
+            pair = rows(out2, k * 32, 32), rows(in2, k * 32, 32)
+        else:
+            pair = rows(out2, 64 + k * 16, 16), rows(in2, 64 + k * 16, 16)
+        send, recv = (send1, recv1) if level == 1 else (send2, recv2)
+        return pltpu.make_async_remote_copy(
+            src_ref=pair[0],
+            dst_ref=pair[1],
+            send_sem=send.at[k],
+            recv_sem=recv.at[k],
+            device_id=(py + dy, px + dx),
+            device_id_type=MESH,
+        )
+
+    def start(level):
+        for k in ORDER:
+            @pl.when(exists(*WAYS[k]))
+            def _():
+                message(level, k).start()
+
+    def receive(level):
+        for k in ORDER:
+            dx, dy = WAYS[k]
+
+            @pl.when(exists(-dx, -dy))
+            def _():
+                message(level, k).wait_recv()
+
+    for k, (dx, dy) in enumerate(WAYS):
         @pl.when(jnp.logical_not(exists(-dx, -dy)))
         def _():
-            in_buf[start:start + size, :] = jnp.zeros((size, 128), jnp.float32)
+            if k < 4:
+                face1_in[k * 32:k * 32 + 32, :] = jnp.zeros((32, 256), jnp.float32)
+                in2[k * 32:k * 32 + 32, :] = jnp.zeros((32, 128), jnp.float32)
+            else:
+                corner1_in[k - 4] = jnp.zeros((4, 256), jnp.float32)
+                in2[64 + k * 16:80 + k * 16, :] = jnp.zeros((16, 128), jnp.float32)
 
     loads[0].wait()
     loads[1].wait()
-    z = dot(x_v[...].reshape(256, 256), t_v[...])
-    z1, z2 = z[:, :256], z[:, 256:]
+    x = x_v[...].reshape(256, 256)
+    z1 = dot(x, t1_v[...])
     loads[2].wait()
     p1 = dot(s1_v[:144, :], z1)
-    loads[3].wait()
-    p2 = dot(s2_v[:192, :], z2)
-    for k in range(4):
-        at = k * FACE
-        out_buf[at:at + 32, :] = p1[k * 32:k * 32 + 32, :128]
-        out_buf[at + 32:at + 64, :] = p1[k * 32:k * 32 + 32, 128:]
-        out_buf[at + 64:at + 96, :] = p2[k * 32:k * 32 + 32, :]
-        at = 4 * FACE + k * CORNER
-        out_buf[at:at + 4, :] = p1[128 + k * 4:132 + k * 4, :128]
-        out_buf[at + 4:at + 8, :] = p1[128 + k * 4:132 + k * 4, 128:]
-        out_buf[at + 8:at + 24, :] = p2[128 + k * 16:144 + k * 16, :]
-
+    face1_out[...] = p1[:128, :]
+    corner1_out[...] = p1[128:144, :].reshape(4, 4, 256)
     pl.semaphore_wait(
         barrier,
         (1 + has_x[1] + has_x[-1]) * (1 + has_y[1] + has_y[-1]) - 1,
     )
-
-    def message(k):
-        (dx, dy), (start, size) = WAYS[k], SLOTS[k]
-        return pltpu.make_async_remote_copy(
-            src_ref=out_buf.at[pl.ds(start, size)],
-            dst_ref=in_buf.at[pl.ds(start, size)],
-            send_sem=send_sem.at[k],
-            recv_sem=recv_sem.at[k],
-            device_id=(py + dy, px + dx),
-            device_id_type=MESH,
-        )
-
-    order = (2, 3, 4, 5, 6, 7, 0, 1)
-    for k in order:
-        @pl.when(exists(*WAYS[k]))
-        def _():
-            message(k).start()
-
+    start(1)
+
+    loads[3].wait()
+    z2 = dot(x, t2_v[...])
+    loads[4].wait()
+    out2[...] = dot(s2_v[:192, :], z2)
+    start(2)
+
+    for load in loads[5:]:
+        load.wait()
     own1 = dot(s1_v[144:, :], z1)
     own2 = dot(s2_v[192:, :], z2)
-    loads[4].wait()
-    loads[5].wait()
-
-    for k in order:
-        dx, dy = WAYS[k]
-
-        @pl.when(exists(-dx, -dy))
-        def _():
-            message(k).wait_recv()
-
-    halo1 = [
-        jnp.concatenate(
-            [in_buf[k * FACE:k * FACE + 32, :], in_buf[k * FACE + 32:k * FACE + 64, :]], axis=1
-        )
-        for k in range(4)
-    ]
-    halo2 = [in_buf[k * FACE + 64:k * FACE + 96, :] for k in range(4)]
-    for k in range(4):
-        at = 4 * FACE + k * CORNER
-        halo1.append(jnp.concatenate([in_buf[at:at + 4, :], in_buf[at + 4:at + 8, :]], axis=1))
-        halo2.append(in_buf[at + 8:at + 24, :])
-    o2 = own2 + dot(u2_v[...], jnp.concatenate(halo2, axis=0))
-    o1 = own1 + dot(u1_v[...], jnp.concatenate(halo1, axis=0))
-
-    o2 = o2.reshape(4, 4, 8, 128)
+
+    receive(1)
+    halo1 = jnp.concatenate([face1_in[...], corner1_in[...].reshape(16, 256)], axis=0)
+    o1 = own1 + dot(u1_v[...], halo1)
+    for band in range(4):
+        for bz in range(2):
+            if band + bz:
+                one[2 * band + bz - 1] = o1[
+                    band * 64:band * 64 + 64, bz * 128:bz * 128 + 128
+                ].reshape(8, 8, 128)
+
+    receive(2)
+    o2 = (own2 + dot(u2_v[...], in2[...])).reshape(4, 4, 8, 128)
     for band in range(4):
         for bz in range(2):
             part = o2[band, :, :4, bz * 64:bz * 64 + 64]
             if band + bz:
                 two[2 * band + bz - 1] = part
-                one[2 * band + bz - 1] = o1[
-                    band * 64:band * 64 + 64, bz * 128:bz * 128 + 128
-                ].reshape(8, 8, 128)
             else:
                 approx[...] = part
 
-    for k in order:
-        @pl.when(exists(*WAYS[k]))
-        def _():
-            message(k).wait_send()
+    for level in (1, 2):
+        for k in ORDER:
+            @pl.when(exists(*WAYS[k]))
+            def _():
+                message(level, k).wait_send()
 
 
 def store(approx_v, two_v, one_v, approx, two, one, sem):
@@ -259,17 +275,20 @@
     results = pl.pallas_call(
         functools.partial(kernel, nx, ny),
         out_shape=tuple(pltpu.VMEM(shape, f32) for shape in shapes),
-        in_specs=[pl.BlockSpec(memory_space=pl.ANY)] * 6,
+        in_specs=[pl.BlockSpec(memory_space=pl.ANY)] * 7,
         out_specs=(vmem, vmem, vmem),
         scratch_shapes=[pltpu.VMEM((bx, by, nz), f32)]
         + tables
         + [
-            pltpu.VMEM((4 * (FACE + CORNER), 128), f32),
-            pltpu.VMEM((4 * (FACE + CORNER), 128), f32),
-            pltpu.SemaphoreType.DMA((6,)),
-            pltpu.SemaphoreType.DMA((8,)),
-            pltpu.SemaphoreType.DMA((8,)),
-        ],
+            pltpu.VMEM((128, 256), f32),
+            pltpu.VMEM((128, 256), f32),
+            pltpu.VMEM((4, 4, 256), f32),
+            pltpu.VMEM((4, 4, 256), f32),
+            pltpu.VMEM((192, 128), f32),
+            pltpu.VMEM((192, 128), f32),
+            pltpu.SemaphoreType.DMA((9,)),
+        ]
+        + [pltpu.SemaphoreType.DMA((8,))] * 4,
         compiler_params=pltpu.CompilerParams(
             collective_id=0, has_side_effects=True, vmem_limit_bytes=60 * 1024 * 1024
         ),

time: 11.4 us -> 11.1 us (0.974)
  Pallas kernels: 10.6 us -> 10.3 us
    pallas_call x1, Pallas kernels: 9.84 us -> 9.59 us  [per_device(): pl.pallas_call(functools.partial(kernel, nx, ny), out_shape=tuple((pltpu....]
where the time goes in v3:
time: 11.1 us; the launch traced here: 11 us
  Pallas kernels  10.3 us (93%)
  between operations  0.64 us (6%)
    pallas_call x1, Pallas kernels, per_device(): pl.pallas_call(functools.partial(kernel, nx, ny), out_shape=tuple((pltpu....  9.59 us
    pallas_call x1, Pallas kernels, per_device(): pl.pallas_call(store, out_shape=tuple((jax.ShapeDtypeStruct(shape, f32) f...  0.73 us

profile of v3, /device:TPU:1, one launch (start us, length us, event | category | flops | bytes accessed | tf_op | source)
XLA Modules:
  0.0 11.0 jit_solution(9174487099558558101)
XLA Ops:
  0.6 9.6 %shard_map.94 = (f32[4,4,64]{2,1,0:T(4,128)S(1)}, f32[7,4,4,64]{3,2,1,0:T(4,128)S(1)}, f32[7,8,8,128]{3,2,1,0:T(8,128)S(1)}) custom-call(f32[16,16,256]{2,1,0:T(8,128)} %x_hbm.1, f32[256,256]{1,0:T(8,128)} %constant.12.clone.t1_hbm, f32[256,128]{1,0:T(8,128)} %constant.13.clone.t2_hbm, f32[9,400,256]{2,1,0:T(8,128)} %constant.14.clone.s1_hbm, ...), custom_call_target="tpu_custom_call" | custom-call | tf_op jit(solution)/shard_map/pallas_call | solution.py:275
  10.2 0.7 %shard_map.95 = (f32[4,4,64]{2,1,0:T(4,128)}, f32[7,4,4,64]{3,2,1,0:T(4,128)}, f32[7,8,8,128]{3,2,1,0:T(8,128)}) custom-call(f32[4,4,64]{2,1,0:T(4,128)S(1)} %get-tuple-element.6.approx_v, f32[7,4,4,64]{3,2,1,0:T(4,128)S(1)} %get-tuple-element.7.two_v, f32[7,8,8,128]{3,2,1,0:T(8,128)S(1)} %get-tuple-element.8.one_v), custom_call_target="tpu_custom_call" | custom-call | tf_op jit(solution)/shard_map/pallas_call | solution.py:297

commit v4 on v3

--- a/solution.py
+++ b/solution.py
@@ -75,45 +75,59 @@
 
 
 @functools.lru_cache(maxsize=None)
-def matrices(bx, by, nz):
+def tables(bx, by, nz):
     low, high = lift_matrix(nz)
     low2, high2 = lift_matrix(nz // 2)
-    depth1 = np.concatenate([low, high]).T.astype(np.float32)
-    depth2 = np.concatenate([low2 @ low, high2 @ low]).T.astype(np.float32)
-    sends, spreads = [], []
-    for level, pad in ((0, 1), (1, 2)):
-        own_x, ux, vx = block_maps(bx)[level]
-        own_y, uy, vy = block_maps(by)[level]
-        nx, ny = own_x[0].shape[0], own_y[0].shape[0]
-        eye_x, eye_y = np.eye(nx), np.eye(ny)
-        spread = [np.kron(ux[dx] if dx else eye_x, uy[dy] if dy else eye_y) for dx, dy in WAYS]
-
-        def by_band(m):
-            m = m.reshape(2, nx // 2, 2, ny // 2, -1).transpose(0, 2, 1, 3, 4)
-            m = np.pad(m, ((0, 0),) * 3 + ((0, (pad - 1) * (ny // 2)), (0, 0)))
-            return m.reshape(-1, m.shape[-1])
-
-        spreads.append(by_band(np.concatenate(spread, 1)).astype(np.float32))
-        rows = []
-        for cx in range(3):
-            for cy in range(3):
-                out = [
-                    np.kron(vx[dx] if dx else own_x[cx], vy[dy] if dy else own_y[cy])
-                    for dx, dy in WAYS
-                ]
-                out.append(by_band(np.kron(own_x[cx], own_y[cy])))
-                rows.append(np.concatenate(out))
-        sends.append(np.stack(rows).astype(np.float32))
-    return depth1, depth2, sends[0], sends[1], spreads[0], spreads[1]
+    depth1 = np.concatenate([low, high]).T
+    depth2 = np.concatenate([low2, high2]).T
+    levels_x, levels_y = block_maps(bx), block_maps(by)
+    own_x, ux, vx = levels_x[1]
+    own_y, uy, vy = levels_y[1]
+    nx, ny = own_x[0].shape[0], own_y[0].shape[0]
+    plane = []
+    for cx in range(3):
+        for cy in range(3):
+            out = []
+            for dx, dy in WAYS:
+                m = np.kron(vx[dx] if dx else own_x[cx], vy[dy] if dy else own_y[cy])
+                if dx == 0:
+                    m = m.reshape(nx, -1, bx * by).transpose(1, 0, 2).reshape(-1, bx * by)
+                out.append(m)
+            out.append(np.kron(own_x[cx], own_y[cy]))
+            plane.append(np.concatenate(out))
+    columns = np.concatenate([u[d].T.reshape(-1) for u in (levels_y[0][1], uy) for d in (1, -1)])
+    columns = np.repeat(columns[:, None], 128, axis=1)
+    arrays = [t.astype(np.float32) for t in (depth1, depth2, np.stack(plane), columns)]
+    return arrays, levels_x, levels_y
 
 
 def dot(a, b):
     return jnp.dot(a, b, precision=HIGHEST, preferred_element_type=jnp.float32)
 
 
+def lift_ends(e, o, prev, after, first, last):
+    at, sub = jnp.where, lambda f, *lists: [f(*v) for v in zip(*lists)]
+    e_after = after(e, sub(lambda p: at(last, p, 0.0), e))
+    d1 = sub(lambda p, q, r: p + LIFT_ALPHA * (q + r), o, e, e_after)
+    out1 = sub(lambda p: LIFT_ALPHA * p, e)
+    d1_prev = prev(d1, sub(lambda p, q: at(first, p, q), d1, out1))
+    s1 = sub(lambda p, q, r: p + LIFT_BETA * (q + r), e, d1_prev, d1)
+    s1_after = after(s1, sub(lambda p, q: at(last, p, LIFT_BETA * q), s1, d1))
+    d2 = sub(lambda p, q, r: p + LIFT_GAMMA * (q + r), d1, s1, s1_after)
+    out2 = sub(lambda p, q: p + LIFT_GAMMA * (LIFT_BETA * p + q), out1, s1)
+    d2_prev = prev(d2, sub(lambda p, q: at(first, p, q), d2, out2))
+    s2 = sub(lambda p, q, r: p + LIFT_DELTA * (q + r), s1, d2_prev, d2)
+    return [v * LIFT_SCALE for v in s2], [v * (1.0 / LIFT_SCALE) for v in d2]
+
+
+def weighted(weights, values):
+    terms = [float(w) * v for w, v in zip(weights, values) if w != 0.0]
+    return functools.reduce(lambda p, q: p + q, terms)
+
+
 def kernel(
-    nx, ny, x_hbm, t1_hbm, t2_hbm, s1_hbm, s2_hbm, u1_hbm, u2_hbm, approx, two, one,
-    x_v, t1_v, t2_v, s1_v, s2_v, u1_v, u2_v,
+    nx, ny, levels_x, levels_y, x_hbm, t1_hbm, t2_hbm, s2_hbm, uy_hbm, approx, two, one,
+    x_v, t1_v, t2_v, s2_v, uy_v, xb, own1,
     face1_out, face1_in, corner1_out, corner1_in, out2, in2,
     load_sem, send1, recv1, send2, recv2,
 ):
@@ -130,19 +144,14 @@
     def rows(ref, start, size):
         return ref.at[pl.ds(start, size)]
 
-    n1, n2 = s1_v.shape[0] - 144, s2_v.shape[0] - 192
     loads = [
         pltpu.make_async_copy(source, target, load_sem.at[k])
         for k, (source, target) in enumerate((
             (x_hbm, x_v),
             (t1_hbm, t1_v),
-            (s1_hbm.at[here, pl.ds(0, 144)], rows(s1_v, 0, 144)),
             (t2_hbm, t2_v),
-            (s2_hbm.at[here, pl.ds(0, 192)], rows(s2_v, 0, 192)),
-            (s1_hbm.at[here, pl.ds(144, n1)], rows(s1_v, 144, n1)),
-            (s2_hbm.at[here, pl.ds(192, n2)], rows(s2_v, 192, n2)),
-            (u1_hbm, u1_v),
-            (u2_hbm, u2_v),
+            (s2_hbm.at[here], s2_v),
+            (uy_hbm, uy_v),
         ))
     ]
     for load in loads:
@@ -202,48 +211,144 @@
 
     loads[0].wait()
     loads[1].wait()
-    x = x_v[...].reshape(256, 256)
-    z1 = dot(x, t1_v[...])
+    z1 = dot(x_v[...].reshape(256, 256), t1_v[...])
+
+    planes = [z1[16 * i:16 * i + 16, :] for i in range(16)]
+    low, high = lift_ends(
+        planes[0::2], planes[1::2],
+        lambda v, end: [end[0]] + v[:-1],
+        lambda v, end: v[1:] + [end[-1]],
+        not_first_x == 0, last_x == 1,
+    )
+    _, ux, vx = levels_x[0]
+    _, uy, vy = levels_y[0]
+    along = [weighted(w, planes) for d in (1, -1) for w in vx[d]]
+    for r, v in enumerate(low + high + along):
+        for h in range(2):
+            xb[320 * h + 16 * r:320 * h + 16 * r + 16, :] = v[:, 128 * h:128 * h + 128]
+
+    def strided(begin, size, stride):
+        return jnp.concatenate(
+            [xb[pl.ds(320 * h + begin, size, stride=stride), :] for h in range(2)], axis=1
+        )
+
+    for kd, d in enumerate((1, -1)):
+        for ky in range(2):
+            taps = [y for y in range(16) if vy[d][ky, y] != 0.0]
+            weights = [vy[d][ky, y] for y in taps]
+            at = (2 + kd) * 32 + ky * 16
+            face1_out[at:at + 16, :] = weighted(
+                weights, [strided(y, 16, 16) for y in taps]
+            )
+            part = weighted(weights, [strided(256 + y, 4, 16) for y in taps])
+            corner1_out[kd, 2 * ky:2 * ky + 2, :] = part[0:2]
+            corner1_out[2 + kd, 2 * ky:2 * ky + 2, :] = part[2:4]
+
+    place = lax.broadcasted_iota(jnp.int32, (8, 256), 0)
+    for r in (16, 17, 18, 19) + tuple(range(16)):
+        low, high = lift_ends(
+            [strided(16 * r, 8, 2)], [strided(16 * r + 1, 8, 2)],
+            lambda v, end: [jnp.where(place == 0, end[0], pltpu.roll(v[0], 1, 0))],
+            lambda v, end: [jnp.where(place == 7, end[0], pltpu.roll(v[0], 7, 0))],
+            not_first_y == 0, last_y == 1,
+        )
+        if r >= 16:
+            at = (r - 16) * 16
+            face1_out[at:at + 8, :] = low[0]
+            face1_out[at + 8:at + 16, :] = high[0]
+        else:
+            own1[r, 0] = low[0]
+            own1[r, 1] = high[0]
+        if r == 19:
+            pl.semaphore_wait(
+                barrier,
+                (1 + has_x[1] + has_x[-1]) * (1 + has_y[1] + has_y[-1]) - 1,
+            )
+            start(1)
+
     loads[2].wait()
-    p1 = dot(s1_v[:144, :], z1)
-    face1_out[...] = p1[:128, :]
-    corner1_out[...] = p1[128:144, :].reshape(4, 4, 256)
-    pl.semaphore_wait(
-        barrier,
-        (1 + has_x[1] + has_x[-1]) * (1 + has_y[1] + has_y[-1]) - 1,
-    )
-    start(1)
-
+    z2 = dot(z1[:, :128], t2_v[...])
     loads[3].wait()
-    z2 = dot(x, t2_v[...])
+    p2 = dot(s2_v[...], z2)
+    out2[...] = p2[:192, :]
+    start(2)
+    own2 = p2[192:, :]
     loads[4].wait()
-    out2[...] = dot(s2_v[:192, :], z2)
-    start(2)
-
-    for load in loads[5:]:
-        load.wait()
-    own1 = dot(s1_v[144:, :], z1)
-    own2 = dot(s2_v[192:, :], z2)
 
     receive(1)
-    halo1 = jnp.concatenate([face1_in[...], corner1_in[...].reshape(16, 256)], axis=0)
-    o1 = own1 + dot(u1_v[...], halo1)
-    for band in range(4):
-        for bz in range(2):
-            if band + bz:
-                one[2 * band + bz - 1] = o1[
-                    band * 64:band * 64 + 64, bz * 128:bz * 128 + 128
-                ].reshape(8, 8, 128)
+    for bz in range(2):
+        half = slice(bz * 128, bz * 128 + 128)
+        column = [[[
+            uy_v[((kd * 2 + ky) * 2 + b) * 8:((kd * 2 + ky) * 2 + b) * 8 + 8, :]
+            for b in range(2)] for ky in range(2)] for kd in range(2)]
+
+        def add_y(value, row, b):
+            for kd in range(2):
+                for ky in range(2):
+                    value = value + row(kd, ky) * column[kd][ky][b]
+            return value
+
+        for b in range(2):
+            side = [
+                [
+                    add_y(
+                        face1_in[dx * 32 + kx * 16 + b * 8:dx * 32 + kx * 16 + b * 8 + 8, half],
+                        lambda kd, ky: corner1_in[dx * 2 + kd, 2 * ky + kx:2 * ky + kx + 1, half],
+                        b,
+                    )
+                    for kx in range(2)
+                ]
+                for dx in range(2)
+            ]
+            for r in range(16):
+                band, i = 2 * (r // 8) + b, r % 8
+                if band + bz == 0:
+                    continue
+                value = add_y(
+                    own1[r, b, :, half],
+                    lambda kd, ky: face1_in[
+                        (2 + kd) * 32 + ky * 16 + r:(2 + kd) * 32 + ky * 16 + r + 1, half
+                    ],
+                    b,
+                )
+                for dx, d in enumerate((1, -1)):
+                    if np.any(ux[d][r] != 0.0):
+                        value = value + weighted(ux[d][r], side[dx])
+                one[2 * band + bz - 1, i] = value
 
     receive(2)
-    o2 = (own2 + dot(u2_v[...], in2[...])).reshape(4, 4, 8, 128)
-    for band in range(4):
-        for bz in range(2):
-            part = o2[band, :, :4, bz * 64:bz * 64 + 64]
-            if band + bz:
-                two[2 * band + bz - 1] = part
-            else:
-                approx[...] = part
+    _, ux2, _ = levels_x[1]
+    column2 = [uy_v[64 + k * 8:72 + k * 8, :] for k in range(8)]
+    side2 = [
+        [
+            in2[dx * 32 + kx * 8:dx * 32 + kx * 8 + 8, :]
+            + sum(
+                in2[at:at + 1, :] * column2[kd * 4 + ky]
+                for kd in range(2)
+                for ky in range(4)
+                for at in (128 + (dx * 2 + kd) * 16 + kx * 4 + ky,)
+            )
+            for kx in range(4)
+        ]
+        for dx in range(2)
+    ]
+    for r in range(8):
+        value = own2[r * 8:r * 8 + 8, :] + sum(
+            in2[at:at + 1, :] * column2[kd * 4 + ky]
+            for kd in range(2)
+            for ky in range(4)
+            for at in ((2 + kd) * 32 + ky * 8 + r,)
+        )
+        for dx, d in enumerate((1, -1)):
+            if np.any(ux2[d][r] != 0.0):
+                value = value + weighted(ux2[d][r], side2[dx])
+        for b in range(2):
+            for bz in range(2):
+                at, part = 4 * (r // 4) + 2 * b + bz, value[4 * b:4 * b + 4, 64 * bz:64 * bz + 64]
+                if at:
+                    two[at - 1, r % 4] = part
+                else:
+                    approx[r % 4] = part
 
     for level in (1, 2):
         for k in ORDER:
@@ -263,30 +368,32 @@
 
 def per_device(nx, ny, velocity):
     bx, by, nz = velocity.shape
-    consts = matrices(bx, by, nz)
+    consts, levels_x, levels_y = tables(bx, by, nz)
     f32 = jnp.float32
     vmem = pl.BlockSpec(memory_space=pltpu.VMEM)
-    tables = [pltpu.VMEM(c.shape[-2:], f32) for c in consts]
+    held = [pltpu.VMEM(c.shape[-2:], f32) for c in consts]
     shapes = (
         (bx // 4, by // 4, nz // 4),
         (7, bx // 4, by // 4, nz // 4),
         (7, bx // 2, by // 2, nz // 2),
     )
     results = pl.pallas_call(
-        functools.partial(kernel, nx, ny),
+        functools.partial(kernel, nx, ny, levels_x, levels_y),
         out_shape=tuple(pltpu.VMEM(shape, f32) for shape in shapes),
-        in_specs=[pl.BlockSpec(memory_space=pl.ANY)] * 7,
+        in_specs=[pl.BlockSpec(memory_space=pl.ANY)] * 5,
         out_specs=(vmem, vmem, vmem),
         scratch_shapes=[pltpu.VMEM((bx, by, nz), f32)]
-        + tables
+        + held
         + [
+            pltpu.VMEM((640, 128), f32),
+            pltpu.VMEM((16, 2, 8, 256), f32),
             pltpu.VMEM((128, 256), f32),
             pltpu.VMEM((128, 256), f32),
             pltpu.VMEM((4, 4, 256), f32),
             pltpu.VMEM((4, 4, 256), f32),
             pltpu.VMEM((192, 128), f32),
             pltpu.VMEM((192, 128), f32),
-            pltpu.SemaphoreType.DMA((9,)),
+            pltpu.SemaphoreType.DMA((5,)),
         ]
         + [pltpu.SemaphoreType.DMA((8,))] * 4,
         compiler_params=pltpu.CompilerParams(

time: 11.1 us -> 9.97 us (0.90)
  Pallas kernels: 10.3 us -> 9.18 us
    pallas_call x1, Pallas kernels: 9.59 us -> 8.45 us  [per_device(): pl.pallas_call(functools.partial(kernel, nx, ny, levels_x, levels_y), out...]
where the time goes in v4:
time: 9.97 us; the launch traced here: 9.82 us
  Pallas kernels  9.18 us (92%)
  between operations  0.64 us (6%)
    pallas_call x1, Pallas kernels, per_device(): pl.pallas_call(functools.partial(kernel, nx, ny, levels_x, levels_y), out...  8.45 us
    pallas_call x1, Pallas kernels, per_device(): pl.pallas_call(store, out_shape=tuple((jax.ShapeDtypeStruct(shape, f32) f...  0.73 us

profile of v4, /device:TPU:1, one launch (start us, length us, event | category | flops | bytes accessed | tf_op | source)
XLA Modules:
  0.0 9.8 jit_solution(11917109531896692457)
XLA Ops:
  0.6 8.5 %shard_map.76 = (f32[4,4,64]{2,1,0:T(4,128)S(1)}, f32[7,4,4,64]{3,2,1,0:T(4,128)S(1)}, f32[7,8,8,128]{3,2,1,0:T(8,128)S(1)}) custom-call(f32[16,16,256]{2,1,0:T(8,128)} %x_hbm.1, f32[256,256]{1,0:T(8,128)} %constant.8.clone.t1_hbm, f32[128,128]{1,0:T(8,128)} %constant.9.clone.t2_hbm, f32[9,256,256]{2,1,0:T(8,128)} %constant.10.clone.s2_hbm, ...), custom_call_target="tpu_custom_call" | custom-call | tf_op jit(solution)/shard_map/pallas_call | solution.py:380
  9.1 0.7 %shard_map.77 = (f32[4,4,64]{2,1,0:T(4,128)}, f32[7,4,4,64]{3,2,1,0:T(4,128)}, f32[7,8,8,128]{3,2,1,0:T(8,128)}) custom-call(f32[4,4,64]{2,1,0:T(4,128)S(1)} %get-tuple-element.6.approx_v, f32[7,4,4,64]{3,2,1,0:T(4,128)S(1)} %get-tuple-element.7.two_v, f32[7,8,8,128]{3,2,1,0:T(8,128)S(1)} %get-tuple-element.8.one_v), custom_call_target="tpu_custom_call" | custom-call | tf_op jit(solution)/shard_map/pallas_call | solution.py:404

commit v5 on v4

--- a/solution.py
+++ b/solution.py
@@ -18,7 +18,7 @@
 FACES = ((1, 0), (-1, 0), (0, 1), (0, -1))
 CORNERS = ((1, 1), (1, -1), (-1, 1), (-1, -1))
 WAYS = FACES + CORNERS
-ORDER = (2, 3, 4, 5, 6, 7, 0, 1)
+ORDER = (4, 5, 6, 7, 0, 1, 2, 3)
 HIGHEST = lax.Precision.HIGHEST
 
 
@@ -212,6 +212,10 @@
     loads[0].wait()
     loads[1].wait()
     z1 = dot(x_v[...].reshape(256, 256), t1_v[...])
+    for load in loads[2:]:
+        load.wait()
+    z2 = dot(z1[:, :128], t2_v[...])
+    p2 = dot(s2_v[...], z2)
 
     planes = [z1[16 * i:16 * i + 16, :] for i in range(16)]
     low, high = lift_ends(
@@ -259,21 +263,15 @@
         else:
             own1[r, 0] = low[0]
             own1[r, 1] = high[0]
-        if r == 19:
-            pl.semaphore_wait(
-                barrier,
-                (1 + has_x[1] + has_x[-1]) * (1 + has_y[1] + has_y[-1]) - 1,
-            )
-            start(1)
-
-    loads[2].wait()
-    z2 = dot(z1[:, :128], t2_v[...])
-    loads[3].wait()
-    p2 = dot(s2_v[...], z2)
+
     out2[...] = p2[:192, :]
+    own2 = p2[192:, :]
+    pl.semaphore_wait(
+        barrier,
+        (1 + has_x[1] + has_x[-1]) * (1 + has_y[1] + has_y[-1]) - 1,
+    )
+    start(1)
     start(2)
-    own2 = p2[192:, :]
-    loads[4].wait()
 
     receive(1)
     for bz in range(2):
@@ -358,7 +356,7 @@
 
 
 def store(approx_v, two_v, one_v, approx, two, one, sem):
-    pairs = ((one_v, one), (two_v, two), (approx_v, approx))
+    pairs = [(one_v.at[k], one.at[k]) for k in range(7)] + [(two_v, two), (approx_v, approx)]
     copies = [pltpu.make_async_copy(a, b, sem.at[k]) for k, (a, b) in enumerate(pairs)]
     for copy in copies:
         copy.start()
@@ -406,7 +404,7 @@
         out_shape=tuple(jax.ShapeDtypeStruct(shape, f32) for shape in shapes),
         in_specs=[vmem] * 3,
         out_specs=[pl.BlockSpec(memory_space=pl.ANY)] * 3,
-        scratch_shapes=[pltpu.SemaphoreType.DMA((3,))],
+        scratch_shapes=[pltpu.SemaphoreType.DMA((9,))],
     )(*results)
 
 

time: 9.97 us -> 10.3 us (1.033)
  Pallas kernels: 9.18 us -> 9.52 us
    pallas_call x1, Pallas kernels: 8.45 us -> 8.74 us  [per_device(): pl.pallas_call(functools.partial(kernel, nx, ny, levels_x, levels_y), out...]
where the time goes in v5:
time: 10.3 us; the launch traced here: 10.2 us
  Pallas kernels  9.52 us (92%)
  between operations  0.64 us (6%)
    pallas_call x1, Pallas kernels, per_device(): pl.pallas_call(functools.partial(kernel, nx, ny, levels_x, levels_y), out...  8.74 us
    pallas_call x1, Pallas kernels, per_device(): pl.pallas_call(store, out_shape=tuple((jax.ShapeDtypeStruct(shape, f32) f...  0.78 us

profile of v5, /device:TPU:1, one launch (start us, length us, event | category | flops | bytes accessed | tf_op | source)
XLA Modules:
  0.0 10.2 jit_solution(3027488753135112622)
XLA Ops:
  0.6 8.7 %shard_map.76 = (f32[4,4,64]{2,1,0:T(4,128)S(1)}, f32[7,4,4,64]{3,2,1,0:T(4,128)S(1)}, f32[7,8,8,128]{3,2,1,0:T(8,128)S(1)}) custom-call(f32[16,16,256]{2,1,0:T(8,128)} %x_hbm.1, f32[256,256]{1,0:T(8,128)} %constant.8.clone.t1_hbm, f32[128,128]{1,0:T(8,128)} %constant.9.clone.t2_hbm, f32[9,256,256]{2,1,0:T(8,128)} %constant.10.clone.s2_hbm, ...), custom_call_target="tpu_custom_call" | custom-call | tf_op jit(solution)/shard_map/pallas_call | solution.py:378
  9.4 0.8 %shard_map.77 = (f32[4,4,64]{2,1,0:T(4,128)}, f32[7,4,4,64]{3,2,1,0:T(4,128)}, f32[7,8,8,128]{3,2,1,0:T(8,128)}) custom-call(f32[4,4,64]{2,1,0:T(4,128)S(1)} %get-tuple-element.6.approx_v, f32[7,4,4,64]{3,2,1,0:T(4,128)S(1)} %get-tuple-element.7.two_v, f32[7,8,8,128]{3,2,1,0:T(8,128)S(1)} %get-tuple-element.8.one_v), custom_call_target="tpu_custom_call" | custom-call | tf_op jit(solution)/shard_map/pallas_call | solution.py:402

commit v6 on v4

--- a/solution.py
+++ b/solution.py
@@ -18,7 +18,7 @@
 FACES = ((1, 0), (-1, 0), (0, 1), (0, -1))
 CORNERS = ((1, 1), (1, -1), (-1, 1), (-1, -1))
 WAYS = FACES + CORNERS
-ORDER = (2, 3, 4, 5, 6, 7, 0, 1)
+ORDER = (7, 3, 5, 1, 6, 0, 2, 4)
 HIGHEST = lax.Precision.HIGHEST
 
 

time: 9.97 us -> 9.63 us (0.966)
  Pallas kernels: 9.18 us -> 8.84 us
    pallas_call x1, Pallas kernels: 8.45 us -> 8.11 us  [per_device(): pl.pallas_call(functools.partial(kernel, nx, ny, levels_x, levels_y), out...]
where the time goes in v6:
time: 9.63 us; the launch traced here: 9.47 us
  Pallas kernels  8.84 us (92%)
  between operations  0.64 us (7%)
    pallas_call x1, Pallas kernels, per_device(): pl.pallas_call(functools.partial(kernel, nx, ny, levels_x, levels_y), out...  8.11 us
    pallas_call x1, Pallas kernels, per_device(): pl.pallas_call(store, out_shape=tuple((jax.ShapeDtypeStruct(shape, f32) f...  0.73 us

profile of v6, /device:TPU:1, one launch (start us, length us, event | category | flops | bytes accessed | tf_op | source)
XLA Modules:
  0.0 9.5 jit_solution(10567456783196643216)
XLA Ops:
  0.6 8.1 %shard_map.76 = (f32[4,4,64]{2,1,0:T(4,128)S(1)}, f32[7,4,4,64]{3,2,1,0:T(4,128)S(1)}, f32[7,8,8,128]{3,2,1,0:T(8,128)S(1)}) custom-call(f32[16,16,256]{2,1,0:T(8,128)} %x_hbm.1, f32[256,256]{1,0:T(8,128)} %constant.8.clone.t1_hbm, f32[128,128]{1,0:T(8,128)} %constant.9.clone.t2_hbm, f32[9,256,256]{2,1,0:T(8,128)} %constant.10.clone.s2_hbm, ...), custom_call_target="tpu_custom_call" | custom-call | tf_op jit(solution)/shard_map/pallas_call | solution.py:380
  8.7 0.7 %shard_map.77 = (f32[4,4,64]{2,1,0:T(4,128)}, f32[7,4,4,64]{3,2,1,0:T(4,128)}, f32[7,8,8,128]{3,2,1,0:T(8,128)}) custom-call(f32[4,4,64]{2,1,0:T(4,128)S(1)} %get-tuple-element.6.approx_v, f32[7,4,4,64]{3,2,1,0:T(4,128)S(1)} %get-tuple-element.7.two_v, f32[7,8,8,128]{3,2,1,0:T(8,128)S(1)} %get-tuple-element.8.one_v), custom_call_target="tpu_custom_call" | custom-call | tf_op jit(solution)/shard_map/pallas_call | solution.py:404

commit v7 on v6

--- a/solution.py
+++ b/solution.py
@@ -18,7 +18,7 @@
 FACES = ((1, 0), (-1, 0), (0, 1), (0, -1))
 CORNERS = ((1, 1), (1, -1), (-1, 1), (-1, -1))
 WAYS = FACES + CORNERS
-ORDER = (7, 3, 5, 1, 6, 0, 2, 4)
+ORDER = (7, 3, 5, 1, 0, 4, 6, 2)
 HIGHEST = lax.Precision.HIGHEST
 
 
@@ -132,11 +132,9 @@
     load_sem, send1, recv1, send2, recv2,
 ):
     px, py = lax.axis_index("slab"), lax.axis_index("morton")
-    not_first_x, last_x = lax.div(px + (nx - 2), nx - 1), lax.div(px, nx - 1)
-    not_first_y, last_y = lax.div(py + (ny - 2), ny - 1), lax.div(py, ny - 1)
-    here = (not_first_x + last_x) * 3 + not_first_y + last_y
-    has_x = {1: 1 - last_x, -1: not_first_x, 0: 1}
-    has_y = {1: 1 - last_y, -1: not_first_y, 0: 1}
+    has_x = {1: jnp.minimum(nx - 1 - px, 1), -1: jnp.minimum(px, 1), 0: 1}
+    has_y = {1: jnp.minimum(ny - 1 - py, 1), -1: jnp.minimum(py, 1), 0: 1}
+    here = (has_x[-1] - has_x[1] + 1) * 3 + has_y[-1] - has_y[1] + 1
 
     def exists(dx, dy):
         return has_x[dx] * has_y[dy] == 1
@@ -147,8 +145,10 @@
     loads = [
         pltpu.make_async_copy(source, target, load_sem.at[k])
         for k, (source, target) in enumerate((
-            (x_hbm, x_v),
-            (t1_hbm, t1_v),
+            (rows(x_hbm, 0, 8), rows(x_v, 0, 8)),
+            (rows(t1_hbm, 0, 128), rows(t1_v, 0, 128)),
+            (rows(x_hbm, 8, 8), rows(x_v, 8, 8)),
+            (rows(t1_hbm, 128, 128), rows(t1_v, 128, 128)),
             (t2_hbm, t2_v),
             (s2_hbm.at[here], s2_v),
             (uy_hbm, uy_v),
@@ -209,8 +209,8 @@
                 corner1_in[k - 4] = jnp.zeros((4, 256), jnp.float32)
                 in2[64 + k * 16:80 + k * 16, :] = jnp.zeros((16, 128), jnp.float32)
 
-    loads[0].wait()
-    loads[1].wait()
+    for load in loads[:4]:
+        load.wait()
     z1 = dot(x_v[...].reshape(256, 256), t1_v[...])
 
     planes = [z1[16 * i:16 * i + 16, :] for i in range(16)]
@@ -218,7 +218,7 @@
         planes[0::2], planes[1::2],
         lambda v, end: [end[0]] + v[:-1],
         lambda v, end: v[1:] + [end[-1]],
-        not_first_x == 0, last_x == 1,
+        px == 0, px == nx - 1,
     )
     _, ux, vx = levels_x[0]
     _, uy, vy = levels_y[0]
@@ -250,7 +250,7 @@
             [strided(16 * r, 8, 2)], [strided(16 * r + 1, 8, 2)],
             lambda v, end: [jnp.where(place == 0, end[0], pltpu.roll(v[0], 1, 0))],
             lambda v, end: [jnp.where(place == 7, end[0], pltpu.roll(v[0], 7, 0))],
-            not_first_y == 0, last_y == 1,
+            py == 0, py == ny - 1,
         )
         if r >= 16:
             at = (r - 16) * 16
@@ -266,14 +266,14 @@
             )
             start(1)
 
-    loads[2].wait()
+    loads[4].wait()
     z2 = dot(z1[:, :128], t2_v[...])
-    loads[3].wait()
+    loads[5].wait()
     p2 = dot(s2_v[...], z2)
     out2[...] = p2[:192, :]
     start(2)
     own2 = p2[192:, :]
-    loads[4].wait()
+    loads[6].wait()
 
     receive(1)
     for bz in range(2):
@@ -315,6 +315,12 @@
                     if np.any(ux[d][r] != 0.0):
                         value = value + weighted(ux[d][r], side[dx])
                 one[2 * band + bz - 1, i] = value
+
+    for level in (1, 2):
+        for k in ORDER:
+            @pl.when(exists(*WAYS[k]))
+            def _():
+                message(level, k).wait_send()
 
     receive(2)
     _, ux2, _ = levels_x[1]
@@ -350,12 +356,6 @@
                 else:
                     approx[r % 4] = part
 
-    for level in (1, 2):
-        for k in ORDER:
-            @pl.when(exists(*WAYS[k]))
-            def _():
-                message(level, k).wait_send()
-
 
 def store(approx_v, two_v, one_v, approx, two, one, sem):
     pairs = ((one_v, one), (two_v, two), (approx_v, approx))
@@ -393,7 +393,7 @@
             pltpu.VMEM((4, 4, 256), f32),
             pltpu.VMEM((192, 128), f32),
             pltpu.VMEM((192, 128), f32),
-            pltpu.SemaphoreType.DMA((5,)),
+            pltpu.SemaphoreType.DMA((7,)),
         ]
         + [pltpu.SemaphoreType.DMA((8,))] * 4,
         compiler_params=pltpu.CompilerParams(

time: 9.63 us -> 9.69 us (level)
  no operation moved by 1% of the time
where the time goes in v7:
time: 9.69 us; the launch traced here: 9.54 us
  Pallas kernels  8.9 us (92%)
  between operations  0.64 us (7%)
    pallas_call x1, Pallas kernels, per_device(): pl.pallas_call(functools.partial(kernel, nx, ny, levels_x, levels_y), out...  8.18 us
    pallas_call x1, Pallas kernels, per_device(): pl.pallas_call(store, out_shape=tuple((jax.ShapeDtypeStruct(shape, f32) f...  0.73 us

profile of v7, /device:TPU:1, one launch (start us, length us, event | category | flops | bytes accessed | tf_op | source)
XLA Modules:
  0.0 9.5 jit_solution(15903323292096615260)
XLA Ops:
  0.6 8.2 %shard_map.76 = (f32[4,4,64]{2,1,0:T(4,128)S(1)}, f32[7,4,4,64]{3,2,1,0:T(4,128)S(1)}, f32[7,8,8,128]{3,2,1,0:T(8,128)S(1)}) custom-call(f32[16,16,256]{2,1,0:T(8,128)} %x_hbm.1, f32[256,256]{1,0:T(8,128)} %constant.8.clone.t1_hbm, f32[128,128]{1,0:T(8,128)} %constant.9.clone.t2_hbm, f32[9,256,256]{2,1,0:T(8,128)} %constant.10.clone.s2_hbm, ...), custom_call_target="tpu_custom_call" | custom-call | tf_op jit(solution)/shard_map/pallas_call | solution.py:380
  8.8 0.7 %shard_map.77 = (f32[4,4,64]{2,1,0:T(4,128)}, f32[7,4,4,64]{3,2,1,0:T(4,128)}, f32[7,8,8,128]{3,2,1,0:T(8,128)}) custom-call(f32[4,4,64]{2,1,0:T(4,128)S(1)} %get-tuple-element.6.approx_v, f32[7,4,4,64]{3,2,1,0:T(4,128)S(1)} %get-tuple-element.7.two_v, f32[7,8,8,128]{3,2,1,0:T(8,128)S(1)} %get-tuple-element.8.one_v), custom_call_target="tpu_custom_call" | custom-call | tf_op jit(solution)/shard_map/pallas_call | solution.py:404

commit v8 on v7

--- a/solution.py
+++ b/solution.py
@@ -76,9 +76,7 @@
 
 @functools.lru_cache(maxsize=None)
 def tables(bx, by, nz):
-    low, high = lift_matrix(nz)
     low2, high2 = lift_matrix(nz // 2)
-    depth1 = np.concatenate([low, high]).T
     depth2 = np.concatenate([low2, high2]).T
     levels_x, levels_y = block_maps(bx), block_maps(by)
     own_x, ux, vx = levels_x[1]
@@ -97,7 +95,7 @@
             plane.append(np.concatenate(out))
     columns = np.concatenate([u[d].T.reshape(-1) for u in (levels_y[0][1], uy) for d in (1, -1)])
     columns = np.repeat(columns[:, None], 128, axis=1)
-    arrays = [t.astype(np.float32) for t in (depth1, depth2, np.stack(plane), columns)]
+    arrays = [t.astype(np.float32) for t in (depth2, np.stack(plane), columns)]
     return arrays, levels_x, levels_y
 
 
@@ -106,7 +104,10 @@
 
 
 def lift_ends(e, o, prev, after, first, last):
-    at, sub = jnp.where, lambda f, *lists: [f(*v) for v in zip(*lists)]
+    def at(grid_end, p, q):
+        return p if grid_end is True else jnp.where(grid_end, p, q)
+
+    sub = lambda f, *lists: [f(*v) for v in zip(*lists)]
     e_after = after(e, sub(lambda p: at(last, p, 0.0), e))
     d1 = sub(lambda p, q, r: p + LIFT_ALPHA * (q + r), o, e, e_after)
     out1 = sub(lambda p: LIFT_ALPHA * p, e)
@@ -126,8 +127,8 @@
 
 
 def kernel(
-    nx, ny, levels_x, levels_y, x_hbm, t1_hbm, t2_hbm, s2_hbm, uy_hbm, approx, two, one,
-    x_v, t1_v, t2_v, s2_v, uy_v, xb, own1,
+    nx, ny, levels_x, levels_y, x_hbm, t2_hbm, s2_hbm, uy_hbm, approx, two, one,
+    x_v, t2_v, s2_v, uy_v, xb, own1,
     face1_out, face1_in, corner1_out, corner1_in, out2, in2,
     load_sem, send1, recv1, send2, recv2,
 ):
@@ -146,9 +147,7 @@
         pltpu.make_async_copy(source, target, load_sem.at[k])
         for k, (source, target) in enumerate((
             (rows(x_hbm, 0, 8), rows(x_v, 0, 8)),
-            (rows(t1_hbm, 0, 128), rows(t1_v, 0, 128)),
             (rows(x_hbm, 8, 8), rows(x_v, 8, 8)),
-            (rows(t1_hbm, 128, 128), rows(t1_v, 128, 128)),
             (t2_hbm, t2_v),
             (s2_hbm.at[here], s2_v),
             (uy_hbm, uy_v),
@@ -209,11 +208,27 @@
                 corner1_in[k - 4] = jnp.zeros((4, 256), jnp.float32)
                 in2[64 + k * 16:80 + k * 16, :] = jnp.zeros((16, 128), jnp.float32)
 
-    for load in loads[:4]:
-        load.wait()
-    z1 = dot(x_v[...].reshape(256, 256), t1_v[...])
-
-    planes = [z1[16 * i:16 * i + 16, :] for i in range(16)]
+    lane = lax.broadcasted_iota(jnp.int32, (16, 128), 1)
+    left = lane < 64
+    cell = 2 * lane
+    to_left = jnp.where(left, cell, cell - 127)
+    to_right = jnp.where(left, cell + 1, cell - 128)
+    planes = []
+    for k in range(2):
+        loads[k].wait()
+        for i in range(8 * k, 8 * k + 8):
+            p = jnp.take_along_axis(x_v[i, :, :128], to_left, axis=1)
+            q = jnp.take_along_axis(x_v[i, :, 128:], to_right, axis=1)
+            low, high = lift_ends(
+                [jnp.where(left, p, q)], [pltpu.roll(jnp.where(left, q, p), 64, 1)],
+                lambda v, end: [jnp.where(lane == 0, end[0], pltpu.roll(v[0], 1, 1))],
+                lambda v, end: [jnp.where(lane == 127, end[0], pltpu.roll(v[0], 127, 1))],
+                True, True,
+            )
+            planes.append(jnp.concatenate([low[0], high[0]], axis=1))
+    loads[2].wait()
+    z2 = dot(jnp.concatenate([p[:, :128] for p in planes], axis=0), t2_v[...])
+
     low, high = lift_ends(
         planes[0::2], planes[1::2],
         lambda v, end: [end[0]] + v[:-1],
@@ -266,14 +281,12 @@
             )
             start(1)
 
-    loads[4].wait()
-    z2 = dot(z1[:, :128], t2_v[...])
-    loads[5].wait()
+    loads[3].wait()
     p2 = dot(s2_v[...], z2)
     out2[...] = p2[:192, :]
     start(2)
     own2 = p2[192:, :]
-    loads[6].wait()
+    loads[4].wait()
 
     receive(1)
     for bz in range(2):
@@ -380,7 +393,7 @@
     results = pl.pallas_call(
         functools.partial(kernel, nx, ny, levels_x, levels_y),
         out_shape=tuple(pltpu.VMEM(shape, f32) for shape in shapes),
-        in_specs=[pl.BlockSpec(memory_space=pl.ANY)] * 5,
+        in_specs=[pl.BlockSpec(memory_space=pl.ANY)] * 4,
         out_specs=(vmem, vmem, vmem),
         scratch_shapes=[pltpu.VMEM((bx, by, nz), f32)]
         + held
@@ -393,7 +406,7 @@
             pltpu.VMEM((4, 4, 256), f32),
             pltpu.VMEM((192, 128), f32),
             pltpu.VMEM((192, 128), f32),
-            pltpu.SemaphoreType.DMA((7,)),
+            pltpu.SemaphoreType.DMA((5,)),
         ]
         + [pltpu.SemaphoreType.DMA((8,))] * 4,
         compiler_params=pltpu.CompilerParams(

time: 9.69 us -> 10.1 us (1.042)
  Pallas kernels: 8.9 us -> 9.36 us
    pallas_call x1, Pallas kernels: 8.18 us -> 8.63 us  [per_device(): pl.pallas_call(functools.partial(kernel, nx, ny, levels_x, levels_y), out...]
where the time goes in v8:
time: 10.1 us; the launch traced here: 10 us
  Pallas kernels  9.36 us (93%)
  between operations  0.64 us (6%)
    pallas_call x1, Pallas kernels, per_device(): pl.pallas_call(functools.partial(kernel, nx, ny, levels_x, levels_y), out...  8.63 us
    pallas_call x1, Pallas kernels, per_device(): pl.pallas_call(store, out_shape=tuple((jax.ShapeDtypeStruct(shape, f32) f...  0.73 us

profile of v8, /device:TPU:1, one launch (start us, length us, event | category | flops | bytes accessed | tf_op | source)
XLA Modules:
  0.0 10.0 jit_solution(5586125298884095029)
XLA Ops:
  0.6 8.6 %shard_map.67 = (f32[4,4,64]{2,1,0:T(4,128)S(1)}, f32[7,4,4,64]{3,2,1,0:T(4,128)S(1)}, f32[7,8,8,128]{3,2,1,0:T(8,128)S(1)}) custom-call(f32[16,16,256]{2,1,0:T(8,128)} %x_hbm.1, f32[128,128]{1,0:T(8,128)} %constant.6.clone.t2_hbm, f32[9,256,256]{2,1,0:T(8,128)} %constant.7.clone.s2_hbm, f32[128,128]{1,0:T(8,128)} %constant.8.clone.uy_hbm), custom_call_target="tpu_custom_call" | custom-call | tf_op jit(solution)/shard_map/pallas_call | solution.py:393
  9.3 0.7 %shard_map.68 = (f32[4,4,64]{2,1,0:T(4,128)}, f32[7,4,4,64]{3,2,1,0:T(4,128)}, f32[7,8,8,128]{3,2,1,0:T(8,128)}) custom-call(f32[4,4,64]{2,1,0:T(4,128)S(1)} %get-tuple-element.6.approx_v, f32[7,4,4,64]{3,2,1,0:T(4,128)S(1)} %get-tuple-element.7.two_v, f32[7,8,8,128]{3,2,1,0:T(8,128)S(1)} %get-tuple-element.8.one_v), custom_call_target="tpu_custom_call" | custom-call | tf_op jit(solution)/shard_map/pallas_call | solution.py:417

commit v9 on v7

--- a/solution.py
+++ b/solution.py
@@ -213,6 +213,9 @@
         load.wait()
     z1 = dot(x_v[...].reshape(256, 256), t1_v[...])
 
+    loads[4].wait()
+    z2 = dot(z1[:, :128], t2_v[...])
+
     planes = [z1[16 * i:16 * i + 16, :] for i in range(16)]
     low, high = lift_ends(
         planes[0::2], planes[1::2],
@@ -265,14 +268,12 @@
                 (1 + has_x[1] + has_x[-1]) * (1 + has_y[1] + has_y[-1]) - 1,
             )
             start(1)
-
-    loads[4].wait()
-    z2 = dot(z1[:, :128], t2_v[...])
-    loads[5].wait()
-    p2 = dot(s2_v[...], z2)
-    out2[...] = p2[:192, :]
-    start(2)
-    own2 = p2[192:, :]
+            loads[5].wait()
+            p2 = dot(s2_v[...], z2)
+            out2[...] = p2[:192, :]
+            start(2)
+            own2 = p2[192:, :]
+
     loads[6].wait()
 
     receive(1)

time: 9.69 us -> 10.1 us (1.042)
  Pallas kernels: 8.9 us -> 9.26 us
    pallas_call x1, Pallas kernels: 8.18 us -> 8.54 us  [per_device(): pl.pallas_call(functools.partial(kernel, nx, ny, levels_x, levels_y), out...]
where the time goes in v9:
time: 10.1 us; the launch traced here: 9.9 us
  Pallas kernels  9.26 us (92%)
  between operations  0.64 us (6%)
    pallas_call x1, Pallas kernels, per_device(): pl.pallas_call(functools.partial(kernel, nx, ny, levels_x, levels_y), out...  8.54 us
    pallas_call x1, Pallas kernels, per_device(): pl.pallas_call(store, out_shape=tuple((jax.ShapeDtypeStruct(shape, f32) f...  0.73 us

profile of v9, /device:TPU:1, one launch (start us, length us, event | category | flops | bytes accessed | tf_op | source)
XLA Modules:
  0.0 9.9 jit_solution(8625226943197907667)
XLA Ops:
  0.6 8.5 %shard_map.76 = (f32[4,4,64]{2,1,0:T(4,128)S(1)}, f32[7,4,4,64]{3,2,1,0:T(4,128)S(1)}, f32[7,8,8,128]{3,2,1,0:T(8,128)S(1)}) custom-call(f32[16,16,256]{2,1,0:T(8,128)} %x_hbm.1, f32[256,256]{1,0:T(8,128)} %constant.8.clone.t1_hbm, f32[128,128]{1,0:T(8,128)} %constant.9.clone.t2_hbm, f32[9,256,256]{2,1,0:T(8,128)} %constant.10.clone.s2_hbm, ...), custom_call_target="tpu_custom_call" | custom-call | tf_op jit(solution)/shard_map/pallas_call | solution.py:381
  9.2 0.7 %shard_map.77 = (f32[4,4,64]{2,1,0:T(4,128)}, f32[7,4,4,64]{3,2,1,0:T(4,128)}, f32[7,8,8,128]{3,2,1,0:T(8,128)}) custom-call(f32[4,4,64]{2,1,0:T(4,128)S(1)} %get-tuple-element.6.approx_v, f32[7,4,4,64]{3,2,1,0:T(4,128)S(1)} %get-tuple-element.7.two_v, f32[7,8,8,128]{3,2,1,0:T(8,128)S(1)} %get-tuple-element.8.one_v), custom_call_target="tpu_custom_call" | custom-call | tf_op jit(solution)/shard_map/pallas_call | solution.py:405

commit v10 on v7

--- a/solution.py
+++ b/solution.py
@@ -79,7 +79,7 @@
     low, high = lift_matrix(nz)
     low2, high2 = lift_matrix(nz // 2)
     depth1 = np.concatenate([low, high]).T
-    depth2 = np.concatenate([low2, high2]).T
+    depth2 = np.concatenate([low2 @ low, high2 @ low]).T
     levels_x, levels_y = block_maps(bx), block_maps(by)
     own_x, ux, vx = levels_x[1]
     own_y, uy, vy = levels_y[1]
@@ -127,7 +127,7 @@
 
 def kernel(
     nx, ny, levels_x, levels_y, x_hbm, t1_hbm, t2_hbm, s2_hbm, uy_hbm, approx, two, one,
-    x_v, t1_v, t2_v, s2_v, uy_v, xb, own1,
+    x_v, t1_v, t2_v, s2_v, uy_v, xb, own1, full,
     face1_out, face1_in, corner1_out, corner1_in, out2, in2,
     load_sem, send1, recv1, send2, recv2,
 ):
@@ -145,13 +145,11 @@
     loads = [
         pltpu.make_async_copy(source, target, load_sem.at[k])
         for k, (source, target) in enumerate((
-            (rows(x_hbm, 0, 8), rows(x_v, 0, 8)),
-            (rows(t1_hbm, 0, 128), rows(t1_v, 0, 128)),
-            (rows(x_hbm, 8, 8), rows(x_v, 8, 8)),
-            (rows(t1_hbm, 128, 128), rows(t1_v, 128, 128)),
+            (x_hbm, x_v),
             (t2_hbm, t2_v),
             (s2_hbm.at[here], s2_v),
             (uy_hbm, uy_v),
+            (t1_hbm, t1_v),
         ))
     ]
     for load in loads:
@@ -209,11 +207,9 @@
                 corner1_in[k - 4] = jnp.zeros((4, 256), jnp.float32)
                 in2[64 + k * 16:80 + k * 16, :] = jnp.zeros((16, 128), jnp.float32)
 
-    for load in loads[:4]:
-        load.wait()
-    z1 = dot(x_v[...].reshape(256, 256), t1_v[...])
-
-    planes = [z1[16 * i:16 * i + 16, :] for i in range(16)]
+    loads[0].wait()
+
+    planes = [x_v[i] for i in range(16)]
     low, high = lift_ends(
         planes[0::2], planes[1::2],
         lambda v, end: [end[0]] + v[:-1],
@@ -266,14 +262,15 @@
             )
             start(1)
 
-    loads[4].wait()
-    z2 = dot(z1[:, :128], t2_v[...])
-    loads[5].wait()
+    loads[1].wait()
+    z2 = dot(x_v[...].reshape(256, 256), t2_v[...])
+    loads[2].wait()
     p2 = dot(s2_v[...], z2)
     out2[...] = p2[:192, :]
     start(2)
     own2 = p2[192:, :]
-    loads[6].wait()
+    loads[3].wait()
+    loads[4].wait()
 
     receive(1)
     for bz in range(2):
@@ -302,8 +299,6 @@
             ]
             for r in range(16):
                 band, i = 2 * (r // 8) + b, r % 8
-                if band + bz == 0:
-                    continue
                 value = add_y(
                     own1[r, b, :, half],
                     lambda kd, ky: face1_in[
@@ -314,7 +309,15 @@
                 for dx, d in enumerate((1, -1)):
                     if np.any(ux[d][r] != 0.0):
                         value = value + weighted(ux[d][r], side[dx])
-                one[2 * band + bz - 1, i] = value
+                full[band * 64 + i * 8:band * 64 + i * 8 + 8, half] = value
+
+    o1 = dot(full[...], t1_v[...])
+    for band in range(4):
+        for bz in range(2):
+            if band + bz:
+                one[2 * band + bz - 1] = o1[
+                    band * 64:band * 64 + 64, bz * 128:bz * 128 + 128
+                ].reshape(8, 8, 128)
 
     for level in (1, 2):
         for k in ORDER:
@@ -387,13 +390,14 @@
         + [
             pltpu.VMEM((640, 128), f32),
             pltpu.VMEM((16, 2, 8, 256), f32),
+            pltpu.VMEM((256, 256), f32),
             pltpu.VMEM((128, 256), f32),
             pltpu.VMEM((128, 256), f32),
             pltpu.VMEM((4, 4, 256), f32),
             pltpu.VMEM((4, 4, 256), f32),
             pltpu.VMEM((192, 128), f32),
             pltpu.VMEM((192, 128), f32),
-            pltpu.SemaphoreType.DMA((7,)),
+            pltpu.SemaphoreType.DMA((5,)),
         ]
         + [pltpu.SemaphoreType.DMA((8,))] * 4,
         compiler_params=pltpu.CompilerParams(

time: 9.69 us -> 9.69 us (level)
  the two profiles are of different devices: /device:TPU:1 before, /device:TPU:0 now
where the time goes in v10:
time: 9.69 us; the launch traced here: 9.54 us
  Pallas kernels  8.9 us (92%)
  between operations  0.64 us (7%)
    pallas_call x1, Pallas kernels, per_device(): pl.pallas_call(functools.partial(kernel, nx, ny, levels_x, levels_y), out...  8.17 us
    pallas_call x1, Pallas kernels, per_device(): pl.pallas_call(store, out_shape=tuple((jax.ShapeDtypeStruct(shape, f32) f...  0.73 us

profile of v10, /device:TPU:0, one launch (start us, length us, event | category | flops | bytes accessed | tf_op | source)
XLA Modules:
  0.0 9.5 jit_solution(4910678843888476055)
XLA Ops:
  0.6 8.2 %shard_map.76 = (f32[4,4,64]{2,1,0:T(4,128)S(1)}, f32[7,4,4,64]{3,2,1,0:T(4,128)S(1)}, f32[7,8,8,128]{3,2,1,0:T(8,128)S(1)}) custom-call(f32[16,16,256]{2,1,0:T(8,128)} %x_hbm.1, f32[256,256]{1,0:T(8,128)} %constant.8.clone.t1_hbm, f32[256,128]{1,0:T(8,128)} %constant.9.clone.t2_hbm, f32[9,256,256]{2,1,0:T(8,128)} %constant.10.clone.s2_hbm, ...), custom_call_target="tpu_custom_call" | custom-call | tf_op jit(solution)/shard_map/pallas_call | solution.py:383
  8.8 0.7 %shard_map.77 = (f32[4,4,64]{2,1,0:T(4,128)}, f32[7,4,4,64]{3,2,1,0:T(4,128)}, f32[7,8,8,128]{3,2,1,0:T(8,128)}) custom-call(f32[4,4,64]{2,1,0:T(4,128)S(1)} %get-tuple-element.6.approx_v, f32[7,4,4,64]{3,2,1,0:T(4,128)S(1)} %get-tuple-element.7.two_v, f32[7,8,8,128]{3,2,1,0:T(8,128)S(1)} %get-tuple-element.8.one_v), custom_call_target="tpu_custom_call" | custom-call | tf_op jit(solution)/shard_map/pallas_call | solution.py:408

commit v11 on v7

--- a/solution.py
+++ b/solution.py
@@ -185,8 +185,8 @@
             device_id_type=MESH,
         )
 
-    def start(level):
-        for k in ORDER:
+    def start(level, ways=ORDER):
+        for k in ways:
             @pl.when(exists(*WAYS[k]))
             def _():
                 message(level, k).start()
@@ -243,6 +243,12 @@
             part = weighted(weights, [strided(256 + y, 4, 16) for y in taps])
             corner1_out[kd, 2 * ky:2 * ky + 2, :] = part[0:2]
             corner1_out[2 + kd, 2 * ky:2 * ky + 2, :] = part[2:4]
+
+    pl.semaphore_wait(
+        barrier,
+        (1 + has_x[1] + has_x[-1]) * (1 + has_y[1] + has_y[-1]) - 1,
+    )
+    start(1, [k for k in ORDER if WAYS[k][1]])
 
     place = lax.broadcasted_iota(jnp.int32, (8, 256), 0)
     for r in (16, 17, 18, 19) + tuple(range(16)):
@@ -260,11 +266,7 @@
             own1[r, 0] = low[0]
             own1[r, 1] = high[0]
         if r == 19:
-            pl.semaphore_wait(
-                barrier,
-                (1 + has_x[1] + has_x[-1]) * (1 + has_y[1] + has_y[-1]) - 1,
-            )
-            start(1)
+            start(1, [k for k in ORDER if not WAYS[k][1]])
 
     loads[4].wait()
     z2 = dot(z1[:, :128], t2_v[...])

time: 9.69 us -> 9.69 us (level)
  no operation moved by 1% of the time
where the time goes in v11:
time: 9.69 us; the launch traced here: 9.54 us
  Pallas kernels  8.91 us (92%)
  between operations  0.64 us (7%)
    pallas_call x1, Pallas kernels, per_device(): pl.pallas_call(functools.partial(kernel, nx, ny, levels_x, levels_y), out...  8.18 us
    pallas_call x1, Pallas kernels, per_device(): pl.pallas_call(store, out_shape=tuple((jax.ShapeDtypeStruct(shape, f32) f...  0.73 us

profile of v11, /device:TPU:1, one launch (start us, length us, event | category | flops | bytes accessed | tf_op | source)
XLA Modules:
  0.0 9.5 jit_solution(17678736299929423040)
XLA Ops:
  0.6 8.2 %shard_map.76 = (f32[4,4,64]{2,1,0:T(4,128)S(1)}, f32[7,4,4,64]{3,2,1,0:T(4,128)S(1)}, f32[7,8,8,128]{3,2,1,0:T(8,128)S(1)}) custom-call(f32[16,16,256]{2,1,0:T(8,128)} %x_hbm.1, f32[256,256]{1,0:T(8,128)} %constant.8.clone.t1_hbm, f32[128,128]{1,0:T(8,128)} %constant.9.clone.t2_hbm, f32[9,256,256]{2,1,0:T(8,128)} %constant.10.clone.s2_hbm, ...), custom_call_target="tpu_custom_call" | custom-call | tf_op jit(solution)/shard_map/pallas_call | solution.py:382
  8.8 0.7 %shard_map.77 = (f32[4,4,64]{2,1,0:T(4,128)}, f32[7,4,4,64]{3,2,1,0:T(4,128)}, f32[7,8,8,128]{3,2,1,0:T(8,128)}) custom-call(f32[4,4,64]{2,1,0:T(4,128)S(1)} %get-tuple-element.6.approx_v, f32[7,4,4,64]{3,2,1,0:T(4,128)S(1)} %get-tuple-element.7.two_v, f32[7,8,8,128]{3,2,1,0:T(8,128)S(1)} %get-tuple-element.8.one_v), custom_call_target="tpu_custom_call" | custom-call | tf_op jit(solution)/shard_map/pallas_call | solution.py:406

commit v12 on v6

--- a/solution.py
+++ b/solution.py
@@ -269,10 +269,9 @@
     loads[2].wait()
     z2 = dot(z1[:, :128], t2_v[...])
     loads[3].wait()
-    p2 = dot(s2_v[...], z2)
-    out2[...] = p2[:192, :]
+    out2[...] = dot(s2_v[:192, :], z2)
     start(2)
-    own2 = p2[192:, :]
+    own2 = dot(s2_v[192:, :], z2)
     loads[4].wait()
 
     receive(1)

time: 9.63 us -> 9.6 us (level)
  no operation moved by 1% of the time
where the time goes in v12:
time: 9.6 us; the launch traced here: 9.45 us
  Pallas kernels  8.81 us (92%)
  between operations  0.64 us (7%)
    pallas_call x1, Pallas kernels, per_device(): pl.pallas_call(functools.partial(kernel, nx, ny, levels_x, levels_y), out...  8.08 us
    pallas_call x1, Pallas kernels, per_device(): pl.pallas_call(store, out_shape=tuple((jax.ShapeDtypeStruct(shape, f32) f...  0.73 us

profile of v12, /device:TPU:1, one launch (start us, length us, event | category | flops | bytes accessed | tf_op | source)
XLA Modules:
  0.0 9.4 jit_solution(7380368578425824177)
XLA Ops:
  0.6 8.1 %shard_map.76 = (f32[4,4,64]{2,1,0:T(4,128)S(1)}, f32[7,4,4,64]{3,2,1,0:T(4,128)S(1)}, f32[7,8,8,128]{3,2,1,0:T(8,128)S(1)}) custom-call(f32[16,16,256]{2,1,0:T(8,128)} %x_hbm.1, f32[256,256]{1,0:T(8,128)} %constant.8.clone.t1_hbm, f32[128,128]{1,0:T(8,128)} %constant.9.clone.t2_hbm, f32[9,256,256]{2,1,0:T(8,128)} %constant.10.clone.s2_hbm, ...), custom_call_target="tpu_custom_call" | custom-call | tf_op jit(solution)/shard_map/pallas_call | solution.py:379
  8.7 0.7 %shard_map.77 = (f32[4,4,64]{2,1,0:T(4,128)}, f32[7,4,4,64]{3,2,1,0:T(4,128)}, f32[7,8,8,128]{3,2,1,0:T(8,128)}) custom-call(f32[4,4,64]{2,1,0:T(4,128)S(1)} %get-tuple-element.6.approx_v, f32[7,4,4,64]{3,2,1,0:T(4,128)S(1)} %get-tuple-element.7.two_v, f32[7,8,8,128]{3,2,1,0:T(8,128)S(1)} %get-tuple-element.8.one_v), custom_call_target="tpu_custom_call" | custom-call | tf_op jit(solution)/shard_map/pallas_call | solution.py:403
